TPU v7x, 512 devices: a whole 4x4x16 slice. The times are simulated.
512 devices in a mesh: ctx: 64 (over z, x), head: 8 (over y, core).
Axes of the slice: x: 4, y: 4, z: 16, core: 2. Of those that a mesh axis runs over, the one named last changes fastest.
Arguments:
- values: float32 [8192, 4096], P('ctx', 'head'), may hold values from -6 to 6
- step_size: float32 [64, 8192], P('head', 'ctx'), may hold values from 7.6293945e-07 to 0.52, as said below
- decay_rate: float32 [64], P('head'), may hold values from -4 to -1, as said below
- input_map: float32 [8192, 128], P('ctx'), may hold values from -3 to 3
- output_map: float32 [8192, 128], P('ctx'), may hold values from -3 to 3
- skip_gain: float32 [64], P('head'), may hold values from 0.5 to 1.5
- grad_output: float32 [8192, 4096], P('ctx', 'head'), may hold values from -6 to 6
Outputs:
- outputs: float32 [8192, 4096], P('ctx', 'head')
- grad_values: float32 [8192, 4096], P('ctx', 'head')
- grad_input_map: float32 [8192, 128], P(('ctx', 'head'))
- grad_output_map: float32 [8192, 128], P(('ctx', 'head'))
Inputs may be any that keep to these rules, and one draw needn't show every extreme that they name: `step_size`: step sizes, each positive. `decay_rate`: decay rates, each negative.
All inputs are finite; a program needn't handle non-finite values.
Results may differ from a plain program's by a relative error of at most 0.0003.
Values sent between devices are 32-bit elements; how exact they have to be, the bound alone decides.
A program may use at most 128 MiB of HBM per device.

v0:
```python
import jax
import jax.numpy as jnp
from jax import lax
from jax.sharding import PartitionSpec as P

GROUP = 128


PRECISE = lax.Precision.HIGHEST


def entering(value, axis, join, neutral, backward):
    count, mine = (lax.axis_size(axis), lax.axis_index(axis))
    pieces = jax.tree.map(lambda part: lax.all_gather(part, axis), value)
    if backward:
        pieces = jax.tree.map(lambda part: part[::-1], pieces)
        mine = count - 1 - mine
    running = jax.tree.map(
        lambda part, zero: jnp.full_like(part, 0) + jnp.asarray(zero, part.dtype), value, neutral
    )

    def lap(position, running):
        longer = join(running, jax.tree.map(lambda part: part[position], pieces))
        return jax.tree.map(lambda new, old: jnp.where(position < mine, new, old), longer, running)

    return lax.fori_loop(0, count - 1, lap, running)


def combine_pair(earlier, later):
    return (earlier[0] * later[0], later[0][:, None, None] * earlier[1] + later[1])


def shards(values, step_size, decay_rate, input_map, output_map, skip_gain, grad_output):
    row_count = values.shape[0]
    head_count = step_size.shape[0]
    head_width = values.shape[1] // head_count
    state_size = input_map.shape[1]
    block_count = row_count // GROUP
    block_values = values.reshape(block_count, GROUP, head_count, head_width)
    block_grads = grad_output.reshape(block_count, GROUP, head_count, head_width)
    block_steps = step_size.reshape(head_count, block_count, GROUP).transpose(1, 0, 2)
    block_inputs = input_map.reshape(block_count, GROUP, state_size)
    block_outputs = output_map.reshape(block_count, GROUP, state_size)
    cumulative = jnp.cumsum(block_steps * decay_rate[None, :, None], axis=2)
    totals = cumulative[:, :, -1]
    running_totals = jnp.cumsum(totals, axis=0)
    before = running_totals - totals
    after = running_totals[-1][None, :] - running_totals
    causal = jnp.arange(GROUP)[:, None] >= jnp.arange(GROUP)[None, :]
    gaps = cumulative[:, :, :, None] - cumulative[:, :, None, :]
    decay = jnp.where(causal, jnp.exp(jnp.where(causal, gaps, 0.0)), 0.0)
    scores = jnp.einsum("ktn,ksn->kts", block_outputs, block_inputs, precision=PRECISE)
    weighted = scores[:, None] * decay
    scaled = block_values * block_steps.transpose(0, 2, 1)[:, :, :, None]
    intersections = jnp.einsum("kthp,kshp->khts", block_grads, scaled, precision=PRECISE) * decay
    end_logs = totals[:, :, None] - cumulative
    to_end = jnp.exp(end_logs)
    from_start = jnp.exp(cumulative)
    block_states = jnp.einsum("kht,ktn,kthp->khnp", to_end, block_inputs, scaled, precision=PRECISE)
    block_adjoints = jnp.einsum(
        "kht,ktn,kthp->khnp", from_start, block_outputs, block_grads, precision=PRECISE
    )
    zero_state = jnp.zeros((head_count, state_size, head_width), jnp.float32)
    carried_in = [zero_state]
    state_sum = jnp.exp(totals[-1])[:, None, None] * carried_in[-1] + block_states[-1]
    carried_out = [zero_state]
    adjoint_sum = block_adjoints[0] + jnp.exp(totals[0])[:, None, None] * carried_out[0]
    carried_in = jnp.stack(carried_in)
    carried_out = jnp.stack(carried_out)
    device_decay = jnp.exp(running_totals[-1])
    local_out = jnp.einsum("khts,kshp->kthp", weighted, scaled, precision=PRECISE)
    local_out = local_out + from_start.transpose(0, 2, 1)[:, :, :, None] * jnp.einsum(
        "ktn,khnp->kthp", block_outputs, carried_in, precision=PRECISE
    )
    local_out = local_out + skip_gain[None, None, :, None] * block_values
    output_grad = jnp.einsum("khts,ksn->ktn", intersections, block_inputs, precision=PRECISE)
    output_grad = output_grad + jnp.einsum(
        "kht,khnp,kthp->ktn", from_start, carried_in, block_grads, precision=PRECISE
    )
    values_grad = jnp.einsum("khst,kshp->kthp", weighted, block_grads, precision=PRECISE)
    values_grad = values_grad + to_end.transpose(0, 2, 1)[:, :, :, None] * jnp.einsum(
        "ktn,khnp->kthp", block_inputs, carried_out, precision=PRECISE
    )
    input_grad = jnp.einsum("khts,ktn->ksn", intersections, block_outputs, precision=PRECISE)
    input_grad = input_grad + jnp.einsum(
        "kht,khnp,kthp->ktn", to_end, carried_out, scaled, precision=PRECISE
    )
    identity = (jnp.ones((head_count,), jnp.float32), zero_state)
    incoming = entering((device_decay, state_sum), "ctx", combine_pair, identity, False)[1]
    entry_weight = jnp.exp(before[:, :, None] + cumulative)
    full_out = local_out + entry_weight.transpose(0, 2, 1)[:, :, :, None] * jnp.einsum(
        "ktn,hnp->kthp", block_outputs, incoming, precision=PRECISE
    )
    output_grad = output_grad + jnp.einsum(
        "kht,hnp,kthp->ktn", entry_weight, incoming, block_grads, precision=PRECISE
    )
    output_grad = output_grad.reshape(row_count, state_size)
    following = entering((device_decay, adjoint_sum), "ctx", combine_pair, identity, True)[1]
    exit_weight = jnp.exp(after[:, :, None] + end_logs)
    values_grad = values_grad + exit_weight.transpose(0, 2, 1)[:, :, :, None] * jnp.einsum(
        "ktn,hnp->kthp", block_inputs, following, precision=PRECISE
    )
    values_grad = (
        block_steps.transpose(0, 2, 1)[:, :, :, None] * values_grad
        + skip_gain[None, None, :, None] * block_grads
    )
    input_grad = input_grad + jnp.einsum(
        "kht,hnp,kthp->ktn", exit_weight, following, scaled, precision=PRECISE
    )
    input_grad = input_grad.reshape(row_count, state_size)
    input_grad_part, output_grad_part = (
        lax.psum_scatter(input_grad, "head", scatter_dimension=0, tiled=True),
        lax.psum_scatter(output_grad, "head", scatter_dimension=0, tiled=True),
    )
    return (
        full_out.reshape(row_count, head_count * head_width),
        values_grad.reshape(row_count, head_count * head_width),
        input_grad_part,
        output_grad_part,
    )


def solution(mesh):
    placed = (
        P("ctx", "head"),
        P("head", "ctx"),
        P("head"),
        P("ctx", None),
        P("ctx", None),
        P("head"),
        P("ctx", "head"),
    )
    return jax.shard_map(
        shards,
        mesh=mesh,
        in_specs=placed,
        out_specs=(
            P("ctx", "head"),
            P("ctx", "head"),
            P(("ctx", "head"), None),
            P(("ctx", "head"), None),
        ),
        check_vma=False,
    )
```

profile of v0, /device:TPU:1, one launch (start us, length us, event | category | flops | bytes accessed | tf_op | source)
XLA Modules:
  0.0 532.4 jit_solution(2188770044687370739)
XLA Ops:
  8.5 1.1 copy.56
  9.6 1.9 fusion.22
  11.6 1.1 copy.47
  12.7 1.8 fusion.20
  14.7 72.1 %all-gather = f32[64,8,1]{1,2,0:T(1,128)S(1)} all-gather(f32[1,8,1]{1,2,0:T(1,128)S(1)} %copy.51), channel_id=2, replica_groups=mesh['ctx'=64,'head'=8] {'ctx'}, dimensions={0}, use_global_device_ids=true | all-gather | bytes 2080 | tf_op jit(solution)/shard_map/all_gather | solution.py:14
  87.5 1.2 fusion.12
  89.3 1.3 convolution_bitcast_fusion.12
  90.6 1.8 fusion.3
  92.4 1.1 fusion.76
  93.5 116.5 %all-gather.6.cloned.1.call-done = f32[64,8,128,64]{2,3,1,0:T(8,128)} async-done(((f32[1,8,128,64]{2,3,1,0:T(8,128)}), f32[64,8,128,64]{2,3,1,0:T(8,128)}) %all-gather.6.cloned.1.call-update) | async-done | bytes 16777232 | tf_op jit(solution)/shard_map/all_gather | solution.py:14
  210.0 11.8 %rev.7 = f32[64,8,128,64]{2,3,1,0:T(8,128)} reverse(f32[64,8,128,64]{2,3,1,0:T(8,128)} %all-gather.6.cloned.1.call-done), dimensions={0} | reverse | bytes 33554432 | tf_op jit(solution)/shard_map/rev | solution.py:16
  221.8 86.0 %while.29 = (s32[]{:T(128)}, f32[8,128,64]{2,1,0:T(8,128)S(1)}, s32[]{:T(128)}, f32[64,8]{1,0:T(8,128)S(1)}, f32[64,8,128,64]{2,3,1,0:T(8,128)}, /*index=5*/s32[]{:T(128)}, s32[]{:T(128)}) while((s32[]{:T(128)}, f32[8,128,64]{2,1,0:T(8,128)S(1)}, s32[]{:T(128)}, f32[64,8]{1,0:T(8,128)S(1)}, f32[64,8,128,64]{2,3,1,0:T(8,128)}, ...), condition=%wide.region_4.5_spmd.clone, body=%wide.region_3.4_spmd.clone.sunk | while | flops 262148 | bytes 1835209 | solution.py:26
  221.8 1.0 constant_dynamic-slice_fusion.5
  223.2 1.0 constant_dynamic-slice_fusion.5
  225.9 1.0 constant_dynamic-slice_fusion.5
  232.7 1.0 constant_dynamic-slice_fusion.5
  235.4 1.0 constant_dynamic-slice_fusion.5
  239.5 1.0 constant_dynamic-slice_fusion.5
  240.9 1.0 constant_dynamic-slice_fusion.5
  245.0 1.0 constant_dynamic-slice_fusion.5
  246.3 1.0 constant_dynamic-slice_fusion.5
  249.1 1.0 constant_dynamic-slice_fusion.5
  251.8 1.0 constant_dynamic-slice_fusion.5
  253.2 1.0 constant_dynamic-slice_fusion.5
  254.5 1.0 constant_dynamic-slice_fusion.5
  255.9 1.0 constant_dynamic-slice_fusion.5
  260.0 1.0 constant_dynamic-slice_fusion.5
  261.3 1.0 constant_dynamic-slice_fusion.5
  262.7 1.0 constant_dynamic-slice_fusion.5
  264.1 1.0 constant_dynamic-slice_fusion.5
  265.4 1.0 constant_dynamic-slice_fusion.5
  268.2 1.0 constant_dynamic-slice_fusion.5
  270.9 1.0 constant_dynamic-slice_fusion.5
  272.3 1.0 constant_dynamic-slice_fusion.5
  277.7 1.0 constant_dynamic-slice_fusion.5
  280.4 1.0 constant_dynamic-slice_fusion.5
  287.2 1.0 constant_dynamic-slice_fusion.5
  294.1 1.0 constant_dynamic-slice_fusion.5
  296.8 1.0 constant_dynamic-slice_fusion.5
  299.5 1.0 constant_dynamic-slice_fusion.5
  300.9 1.0 constant_dynamic-slice_fusion.5
  303.7 1.0 constant_dynamic-slice_fusion.5
  306.4 1.0 constant_dynamic-slice_fusion.5
  307.7 1.0 fusion.5
  308.7 1.2 fusion.18
  310.8 1.0 convolution_bitcast_fusion.10
  312.8 91.0 %all-gather.4.cloned.1.call-done = f32[64,8,128,64]{2,3,1,0:T(8,128)} async-done(((f32[1,8,128,64]{2,3,1,0:T(8,128)}), f32[64,8,128,64]{2,3,1,0:T(8,128)}) %all-gather.4.cloned.1.call-update) | async-done | bytes 16777232 | tf_op jit(solution)/shard_map/all_gather | solution.py:14
  403.7 85.8 %while.28 = (s32[]{:T(128)}, f32[8,128,64]{2,1,0:T(8,128)S(1)}, s32[]{:T(128)}, f32[64,8]{1,0:T(8,128)S(1)}, f32[64,8,128,64]{2,3,1,0:T(8,128)}, /*index=5*/s32[]{:T(128)}, s32[]{:T(128)}) while((s32[]{:T(128)}, f32[8,128,64]{2,1,0:T(8,128)S(1)}, s32[]{:T(128)}, f32[64,8]{1,0:T(8,128)S(1)}, f32[64,8,128,64]{2,3,1,0:T(8,128)}, ...), condition=%wide.region_2.3_spmd.clone, body=%wide.region_1.2_spmd.clone.sunk | while | flops 262148 | bytes 1835209 | solution.py:26
  409.2 1.0 constant_dynamic-slice_fusion.4
  416.0 1.0 constant_dynamic-slice_fusion.4
  418.7 1.0 constant_dynamic-slice_fusion.4
  420.1 1.0 constant_dynamic-slice_fusion.4
  422.8 1.0 constant_dynamic-slice_fusion.4
  424.2 1.0 constant_dynamic-slice_fusion.4
  425.5 1.0 constant_dynamic-slice_fusion.4
  428.3 1.0 constant_dynamic-slice_fusion.4
  431.0 1.0 constant_dynamic-slice_fusion.4
  433.7 1.0 constant_dynamic-slice_fusion.4
  436.5 1.0 constant_dynamic-slice_fusion.4
  439.2 1.0 constant_dynamic-slice_fusion.4
  440.5 1.0 constant_dynamic-slice_fusion.4
  489.6 1.0 convolution_bitcast_fusion.9
  491.5 1.0 fusion.7
  494.1 31.7 %reduce-scatter.5.cloned.1.call-done = f32[16,128]{1,0:T(8,128)} async-done(((f32[128,128]{1,0:T(8,128)}), f32[16,128]{1,0:T(8,128)}) %reduce-scatter.5.cloned.1.call-update) | async-done | bytes 8208 | tf_op jit(solution)/shard_map/reduce_scatter | solution.py:113
  (497 shorter events, 130.4 us)
Async XLA Ops:
  7.2 5.5 %copy-start = (f32[128,128]{1,0:T(8,128)S(1)}, f32[128,128]{1,0:T(8,128)}, u32[]{:S(2)}) copy-start(f32[128,128]{1,0:T(8,128)} %param.14) | copy-start | bytes 196612
  7.2 202.8 %all-gather.6.cloned.1.call-start = ((), (), s32[]{:S(2)}) async-start(), calls=%async_computation.3 | async-start | bytes 17039360 | tf_op jit(solution)/shard_map/all_gather | solution.py:14
  11.6 392.2 %all-gather.4.cloned.1.call-start = ((), (), s32[]{:S(2)}) async-start(), calls=%async_computation.2 | async-start | bytes 17039360 | tf_op jit(solution)/shard_map/all_gather | solution.py:14
  14.5 479.6 %reduce-scatter.3.cloned.1.call-start = ((), (), s32[]{:S(2)}) async-start(), calls=%async_computation.4 | async-start | bytes 73728 | tf_op jit(solution)/shard_map/reduce_scatter | solution.py:112
  93.5 215.3 %copy-start.2 = (f32[8,128]{1,0:T(8,128)S(1)}, f32[8,128]{1,0:T(8,128)}, u32[]{:S(2)}) copy-start(f32[8,128]{1,0:T(8,128)} %param.12) | copy-start | bytes 12292
  93.5 215.3 %copy-start.3 = (f32[8]{0:T(128)S(1)}, f32[8]{0:T(128)}, u32[]{:S(2)}) copy-start(f32[8]{0:T(128)} %param.16) | copy-start | bytes 100
  221.8 90.1 %copy-start.1 = (f32[128,128]{1,0:T(8,128)S(1)}, f32[128,128]{1,0:T(8,128)}, u32[]{:S(2)}) copy-start(f32[128,128]{1,0:T(8,128)} %param.15) | copy-start | bytes 196612
  312.7 213.1 %reduce-scatter.5.cloned.1.call-start = ((), (), s32[]{:S(2)}) async-start(), calls=%async_computation.5 | async-start | bytes 73728 | tf_op jit(solution)/shard_map/reduce_scatter | solution.py:113
Sparse Core Ops, SparseCore 0:
  11.7 198.2 all-gather.5
  213.5 190.1 all-gather.3
  407.1 33.1 reduce-scatter.2
  492.6 33.1 reduce-scatter.4
where the time goes:
time: 537 us; the launch traced here: 532 us
  waiting for transfers between devices  239 us (45%)
  local copies, waits for them, and re-layouts  165 us (31%)
  blocking collectives  72.1 us (13%)
  other arithmetic  18.2 us (3%)
  matrix products  17.7 us (3%)
  between operations  14 us (3%)
  loops' own time  5.56 us (1%)
    all_gather x2, waiting for transfers between devices, entering(): pieces = jax.tree.map(lambda part: lax.all_gather(part, axis), value)  208 us
    dynamic_slice x252, local copies, waits for them, and re-layouts, lap(): longer = join(running, jax.tree.map(lambda part: part[position], pieces))  148 us
    all_gather x1, blocking collectives, entering(): pieces = jax.tree.map(lambda part: lax.all_gather(part, axis), value)  72.1 us
    reduce_scatter x1, waiting for transfers between devices, shards(): lax.psum_scatter(output_grad, 'head', scatter_dimension=0, tiled=True)  31.7 us
    select_n x126, other arithmetic, lap(): jnp.where(position < mine, new, old)  16.8 us
    rev x2, local copies, waits for them, and re-layouts, entering(): pieces = jax.tree.map(lambda part: part[::-1], pieces)  11.8 us
  transfers between devices with their start and end apart: 4, of which 3 were waited for; matrix products, arithmetic and copies ran while one was open for 37% of the time, Pallas kernels for 0%

commit v1 on v0

v1 whole, which is shorter than its diff:
```python
import functools

import jax
import jax.numpy as jnp
from jax import lax
from jax.experimental import pallas as pl
from jax.experimental.pallas import tpu as pltpu
from jax.sharding import PartitionSpec as P

MESH = pl.DeviceIdType.MESH
F32, BF16 = jnp.float32, jnp.bfloat16
NX, NZ, NH = 4, 16, 8
FAR_Z = (8, 7, 9, 6, 10, 5, 11, 4, 12, 3, 13, 2, 14, 1, 15)
FAR_X = (2, 1, 3)
FAR_H = (4, 5, 3, 6, 2, 7, 1)
NN = (((1,), (0,)), ((), ()))
NT = (((1,), (1,)), ((), ()))


def split(x):
    high = x.astype(BF16)
    return high, (x - high.astype(F32)).astype(BF16)


def dot3(a, b, dims=NN):
    (ah, al), (bh, bl) = a, b
    one = functools.partial(lax.dot_general, dimension_numbers=dims, preferred_element_type=F32)
    return one(ah, bh) + (one(al, bh) + one(ah, bl))


def core_kernel(
    v_hbm, step_hbm, rate, b_hbm, c_hbm, gain, g_hbm,
    out_hbm, gv_hbm, maps_out,
    v, g, step, bmap, cmap,
    out_acc, gv_acc, from_w, end_w, gf_h, gf_l, xe_h, xe_l, local_maps,
    xs_f, xs_b, xr_f, xr_b, zs_f, zs_b, zr_f, zr_b, ys_f, ys_b, enter, leave, ws_f, ws_b, inc, fol, rs_s, rs_r,
    load_sem, x1_s, x1_r, z1_s, z1_r, z2_s, z2_r, x2_s, x2_r, rs_ss, rs_rs, out_sem,
):
    ctx, head = lax.axis_index("ctx"), lax.axis_index("head")
    mz, mx = ctx // NX, ctx % NX

    def at_x(d):
        return (mz * NX + lax.rem(mx + d, NX), head)

    def at_z(d):
        return (lax.rem(mz + d, NZ) * NX + mx, head)

    def at_h(d):
        return (ctx, lax.rem(head + d, NH))

    barrier = pltpu.get_barrier_semaphore()
    partners = [at_z(d) for d in FAR_Z] + [at_h(d) for d in FAR_H] + [at_x(d) for d in FAR_X]
    for partner in partners:
        pl.semaphore_signal(barrier, inc=1, device_id=partner, device_id_type=MESH)

    loads = [
        pltpu.make_async_copy(src, dst, load_sem.at[i])
        for i, (src, dst) in enumerate(
            ((step_hbm, step), (b_hbm, bmap), (c_hbm, cmap), (v_hbm, v), (g_hbm, g))
        )
    ]
    for load in loads:
        load.start()

    rows = lax.broadcasted_iota(jnp.int32, (128, 128), 0)
    lanes = lax.broadcasted_iota(jnp.int32, (128, 128), 1)
    first = lanes < 64
    lower = rows >= lanes
    upper = rows <= lanes

    loads[0].wait()
    steps = step[...]
    head_rows = lax.broadcasted_iota(jnp.int32, (NH, 128), 0)
    rates = jnp.zeros((NH, 128), F32)
    for h in range(NH):
        rates = jnp.where(head_rows == h, rate[h], rates)
    cum = lax.dot_general(
        steps * rates, jnp.where(upper, 1.0, 0.0).astype(F32), NN,
        precision=lax.Precision.HIGHEST, preferred_element_type=F32,
    )
    total = cum[:, 127:128]
    table = jnp.concatenate([steps, jnp.exp(cum), jnp.exp(total - cum), cum] + [jnp.zeros((96, 128), F32)], axis=0)
    table = table.T

    def column(kind, h):
        k = kind * NH + h
        return jnp.broadcast_to(table[:, k : k + 1], (128, 128))

    def pair(kind, q):
        return jnp.where(first, column(kind, 2 * q), column(kind, 2 * q + 1))

    loads[1].wait()
    loads[2].wait()
    b_all, c_all = bmap[...], cmap[...]
    b2, c2 = split(b_all), split(c_all)
    bt2, ct2 = split(b_all.T), split(c_all.T)
    loads[3].wait()
    loads[4].wait()

    scaled = []
    for q in range(NX):
        cols = slice(q * 128, (q + 1) * 128)
        step_w, start, end = pair(0, q), pair(1, q), pair(2, q)
        vq, gq = v[:, cols], g[:, cols]
        x = vq * step_w
        scaled.append(x)
        xe, gf = split(x * end), split(gq * start)
        xe_h[q], xe_l[q] = xe
        gf_h[q], gf_l[q] = gf
        from_w[q] = start
        end_w[q] = end * step_w
        xs_f[q, 0:128, :] = dot3(bt2, xe)
        xs_f[q, 128:129, :] = start[127:128, :]
        xs_b[q] = dot3(ct2, gf)

    scores, scores_t = dot3(c2, b2, NT), dot3(b2, c2, NT)
    inner = jnp.zeros((128, 128), F32)
    for q in range(NX):
        cols = slice(q * 128, (q + 1) * 128)
        x, gq = scaled[q], g[:, cols]
        x2, g2 = split(x), split(gq)
        outs, grads = [], []
        for k in range(2):
            h = 2 * q + k
            mine = first if k == 0 else jnp.logical_not(first)
            gap = column(3, h) - cum[h : h + 1, :]
            decay = jnp.exp(jnp.where(lower, gap, -gap))
            below = jnp.where(lower, decay, 0.0)
            above = jnp.where(upper, decay, 0.0)
            part = split(jnp.where(mine, gq, 0.0))
            inner = inner + dot3(part, x2, NT) * below
            outs.append(dot3(split(scores * below), x2))
            grads.append(dot3(split(scores_t * above), g2))
        skip = jnp.where(first[0:1], gain[2 * q], gain[2 * q + 1])
        step_w = pair(0, q)
        out_acc[q] = jnp.where(first, outs[0], outs[1]) + skip * v[:, cols]
        gv_acc[q] = step_w * jnp.where(first, grads[0], grads[1]) + skip * gq
    local_maps[0] = dot3(split(inner), b2)
    local_maps[1] = dot3(split(inner.T), c2)

    pl.semaphore_wait(barrier, len(partners))

    def send(src, dst, send_sem, recv_sem, partner):
        copy = pltpu.make_async_remote_copy(
            src_ref=src, dst_ref=dst, send_sem=send_sem, recv_sem=recv_sem, device_id=partner, device_id_type=MESH
        )
        copy.start()
        return copy

    sent = []

    x1 = []
    for i, (source, target) in enumerate(((xs_f, xr_f), (xs_b, xr_b))):
        x1.append([
            send(source.at[lax.rem(mx + d, NX)], target.at[mx], x1_s.at[i, d - 1], x1_r.at[i, d - 1], at_x(d))
            for d in FAR_X
        ])
        target[mx] = source[mx]
    sent += x1[0] + x1[1]

    z1 = []
    for copy in x1[0]:
        copy.wait_recv()
    decays = [xr_f[k, 128:129, :] for k in range(NX)]
    acc = xr_f[0, 0:128, :]
    for k in range(1, NX):
        acc = acc * decays[k] + xr_f[k, 0:128, :]
    plane = decays[0] * decays[1] * decays[2] * decays[3]
    for j in range(NZ):
        zs_f[j, 0:8, :] = acc[8 * j : 8 * j + 8, :]
        zs_f[j, 8:9, :] = plane
    z1.append([
        send(zs_f.at[lax.rem(mz + d, NZ)], zr_f.at[mz], z1_s.at[0, d - 1], z1_r.at[0, d - 1], at_z(d)) for d in FAR_Z
    ])
    zr_f[mz] = zs_f[mz]
    for copy in x1[1]:
        copy.wait_recv()
    acc = xr_b[NX - 1]
    for k in range(NX - 2, -1, -1):
        acc = acc * decays[k] + xr_b[k]
    for j in range(NZ):
        zs_b[j] = acc[8 * j : 8 * j + 8, :]
    z1.append([
        send(zs_b.at[lax.rem(mz + d, NZ)], zr_b.at[mz], z1_s.at[1, d - 1], z1_r.at[1, d - 1], at_z(d)) for d in FAR_Z
    ])
    zr_b[mz] = zs_b[mz]
    sent += z1[0] + z1[1]

    z2 = []
    mine_rows = pl.ds(pl.multiple_of(mz * 8, 8), 8)
    for copy in z1[0]:
        copy.wait_recv()
    carry = jnp.zeros((8, 128), F32)
    for j in range(NZ):
        ys_f[j] = carry
        carry = carry * zr_f[j, 8:9, :] + zr_f[j, 0:8, :]
    z2.append([
        send(ys_f.at[lax.rem(mz + d, NZ)], enter.at[mine_rows], z2_s.at[0, d - 1], z2_r.at[0, d - 1], at_z(d))
        for d in FAR_Z
    ])
    enter[mine_rows, :] = ys_f[mz]
    for copy in z1[1]:
        copy.wait_recv()
    carry = jnp.zeros((8, 128), F32)
    for j in range(NZ - 1, -1, -1):
        ys_b[j] = carry
        carry = carry * zr_f[j, 8:9, :] + zr_b[j]
    z2.append([
        send(ys_b.at[lax.rem(mz + d, NZ)], leave.at[mine_rows], z2_s.at[1, d - 1], z2_r.at[1, d - 1], at_z(d))
        for d in FAR_Z
    ])
    leave[mine_rows, :] = ys_b[mz]
    sent += z2[0] + z2[1]

    x2 = []
    for copy in z2[0]:
        copy.wait_recv()
    carry = enter[...]
    for k in range(NX):
        ws_f[k] = carry
        if k < NX - 1:
            carry = carry * decays[k] + xr_f[k, 0:128, :]
    x2.append([
        send(ws_f.at[lax.rem(mx + d, NX)], inc.at[mx], x2_s.at[0, d - 1], x2_r.at[0, d - 1], at_x(d)) for d in FAR_X
    ])
    inc[mx] = ws_f[mx]
    for copy in z2[1]:
        copy.wait_recv()
    carry = leave[...]
    for k in range(NX - 1, -1, -1):
        ws_b[k] = carry
        if k > 0:
            carry = carry * decays[k] + xr_b[k]
    x2.append([
        send(ws_b.at[lax.rem(mx + d, NX)], fol.at[mx], x2_s.at[1, d - 1], x2_r.at[1, d - 1], at_x(d)) for d in FAR_X
    ])
    fol[mx] = ws_b[mx]
    sent += x2[0] + x2[1]

    rs, stores = [], []
    plans = (
        (inc, c2, gf_h, gf_l, from_w, out_acc, out_hbm),
        (fol, b2, xe_h, xe_l, end_w, gv_acc, gv_hbm),
    )
    for i, (carried, map2, w_h, w_l, weight, acc_ref, hbm) in enumerate(plans):
        for copy in x2[i]:
            copy.wait_recv()
        grad = local_maps[i]
        for q in range(NX):
            state2 = split(carried[q])
            acc_ref[q] = acc_ref[q] + weight[q] * dot3(map2, state2)
            grad = grad + dot3((w_h[q], w_l[q]), state2, NT)
            store = pltpu.make_async_copy(acc_ref.at[q], hbm.at[:, pl.ds(q * 128, 128)], out_sem.at[i, q])
            store.start()
            stores.append(store)
        for k in range(NH):
            rs_s[i, k] = grad[16 * k : 16 * k + 16, :]
        rs.append([
            send(rs_s.at[i, lax.rem(head + d, NH)], rs_r.at[i, head], rs_ss.at[i, d - 1], rs_rs.at[i, d - 1], at_h(d))
            for d in FAR_H
        ])
        rs_r[i, head] = rs_s[i, head]
    sent += rs[0] + rs[1]
    for i in range(2):
        for copy in rs[i]:
            copy.wait_recv()
        whole = rs_r[i, 0]
        for k in range(1, NH):
            whole = whole + rs_r[i, k]
        maps_out[i] = whole
    for copy in stores:
        copy.wait()
    for copy in sent:
        copy.wait_send()


def hand_kernel(out_in, gv_in, maps_in, out, gv, gi, go, sem):
    copies = [
        pltpu.make_async_copy(src, dst, sem.at[i])
        for i, (src, dst) in enumerate(((out_in, out), (gv_in, gv), (maps_in.at[1], gi), (maps_in.at[0], go)))
    ]
    for copy in copies:
        copy.start()
    for copy in copies:
        copy.wait()


def shards(values, step_size, decay_rate, input_map, output_map, skip_gain, grad_output):
    anywhere = pl.BlockSpec(memory_space=pl.ANY)
    scalars = pl.BlockSpec(memory_space=pltpu.SMEM)
    vmem = lambda *shape, dtype=F32: pltpu.VMEM(shape, dtype)
    dma = lambda *shape: pltpu.SemaphoreType.DMA(shape)
    full = jax.ShapeDtypeStruct(values.shape, F32)
    out, gv, maps = pl.pallas_call(
        core_kernel,
        name="scan_core",
        out_shape=(full, full, jax.ShapeDtypeStruct((2, 16, 128), F32)),
        in_specs=[anywhere, anywhere, scalars, anywhere, anywhere, scalars, anywhere],
        out_specs=(anywhere, anywhere, pl.BlockSpec(memory_space=pltpu.VMEM)),
        scratch_shapes=[
            vmem(128, 512), vmem(128, 512), vmem(8, 128), vmem(128, 128), vmem(128, 128),
            vmem(4, 128, 128), vmem(4, 128, 128), vmem(4, 128, 128), vmem(4, 128, 128),
            vmem(4, 128, 128, dtype=BF16), vmem(4, 128, 128, dtype=BF16),
            vmem(4, 128, 128, dtype=BF16), vmem(4, 128, 128, dtype=BF16), vmem(2, 128, 128),
            vmem(4, 129, 128), vmem(4, 128, 128), vmem(4, 129, 128), vmem(4, 128, 128),
            vmem(16, 9, 128), vmem(16, 8, 128), vmem(16, 9, 128), vmem(16, 8, 128),
            vmem(16, 8, 128), vmem(16, 8, 128), vmem(128, 128), vmem(128, 128),
            vmem(4, 128, 128), vmem(4, 128, 128), vmem(4, 128, 128), vmem(4, 128, 128),
            vmem(2, 8, 16, 128), vmem(2, 8, 16, 128),
            dma(5), dma(2, 3), dma(2, 3), dma(2, 15), dma(2, 15), dma(2, 15), dma(2, 15), dma(2, 3), dma(2, 3),
            dma(2, 7), dma(2, 7), dma(2, 4),
        ],
        compiler_params=pltpu.CompilerParams(
            collective_id=0, has_side_effects=True, vmem_limit_bytes=32 * 1024 * 1024
        ),
    )(values, step_size, decay_rate, input_map, output_map, skip_gain, grad_output)
    piece = jax.ShapeDtypeStruct((16, 128), F32)
    return pl.pallas_call(
        hand_kernel,
        name="hand_over",
        out_shape=(full, full, piece, piece),
        in_specs=[anywhere] * 3,
        out_specs=(anywhere,) * 4,
        scratch_shapes=[pltpu.SemaphoreType.DMA((4,))],
    )(out, gv, maps)


def solution(mesh):
    placed = (
        P("ctx", "head"),
        P("head", "ctx"),
        P("head"),
        P("ctx", None),
        P("ctx", None),
        P("head"),
        P("ctx", "head"),
    )
    return jax.shard_map(
        shards,
        mesh=mesh,
        in_specs=placed,
        out_specs=(
            P("ctx", "head"),
            P("ctx", "head"),
            P(("ctx", "head"), None),
            P(("ctx", "head"), None),
        ),
        check_vma=False,
    )
```

time: 537 us -> 78.7 us (0.15)
  waiting for transfers between devices: 239 us -> 0 us
  local copies, waits for them, and re-layouts: 165 us -> 7.58 us
  blocking collectives: 72.1 us -> 0 us
  Pallas kernels: 0 us -> 70.1 us
  other arithmetic: 18.2 us -> 0 us
  matrix products: 17.7 us -> 0 us
  between operations: 14 us -> 0.67 us
  loops' own time: 5.56 us -> 0 us
    all_gather x2 -> x0, waiting for transfers between devices: 208 us -> none  [entering(): pieces = jax.tree.map(lambda part: lax.all_gather(part, axis), value)]
    dynamic_slice x252 -> x0, local copies, waits for them, and re-layouts: 148 us -> none  [lap(): longer = join(running, jax.tree.map(lambda part: part[position], pieces))]
    all_gather x1 -> x0, blocking collectives: 72.1 us -> none  [entering(): pieces = jax.tree.map(lambda part: lax.all_gather(part, axis), value)]
    pallas_call x0 -> x2, Pallas kernels: none -> 70.1 us  [the longest x1 52.6 us: shards(): pl.pallas_call(core_kernel, name='scan_core', out_shape=(full, full, jax....]
    reduce_scatter x2 -> x0, waiting for transfers between devices: 31.7 us -> none  [the longest x1 31.7 us: shards(): lax.psum_scatter(output_grad, 'head', scatter_dimension=0, tiled=True)]
    dot_general x16 -> x0, matrix products: 17.7 us -> none  [the longest x1 1.91 us: shards(): jnp.einsum('kht,ktn,kthp->khnp', from_start, block_outputs, block_grads,...]
    select_n x126 -> x0, other arithmetic: 16.8 us -> none  [lap(): jnp.where(position < mine, new, old)]
    rev x2 -> x0, local copies, waits for them, and re-layouts: 11.8 us -> none  [entering(): pieces = jax.tree.map(lambda part: part[::-1], pieces)]
  transfers between devices with their start and end apart: 4 -> 0, of which waited for: 3 -> 0; matrix products, arithmetic and copies ran while one was open for 37% -> 0% of each run, Pallas kernels for 0% -> 0%
where the time goes in v1:
time: 78.7 us; the launch traced here: 78.3 us
  Pallas kernels  70.1 us (89%)
  local copies, waits for them, and re-layouts  7.58 us (10%)
    pallas_call x1, Pallas kernels, shards(): pl.pallas_call(core_kernel, name='scan_core', out_shape=(full, full, jax....  52.6 us
    pallas_call x1, Pallas kernels, shards(): pl.pallas_call(hand_kernel, name='hand_over', out_shape=(full, full, piec...  17.5 us
    unnamed x20, local copies, waits for them, and re-layouts  7.58 us

profile of v1, /device:TPU:1, one launch (start us, length us, event | category | flops | bytes accessed | tf_op | source)
XLA Modules:
  0.0 78.3 jit_solution(7144925375946182960)
XLA Ops:
  0.6 0.0 copy-start
  0.6 0.9 %copy-done = f32[128,512]{1,0:T(8,128)S(1)} copy-done((f32[128,512]{1,0:T(8,128)S(1)}, f32[128,512]{1,0:T(8,128)}, u32[]{:S(2)}) %copy-start) | copy-done | bytes 262168
  1.6 0.0 copy-start.1
  1.6 0.9 %copy-done.1 = f32[128,512]{1,0:T(8,128)S(1)} copy-done((f32[128,512]{1,0:T(8,128)S(1)}, f32[128,512]{1,0:T(8,128)}, u32[]{:S(2)}) %copy-start.1) | copy-done | bytes 262168
  2.5 0.0 copy-start.4
  2.5 0.8 %copy-done.4 = f32[128,128]{1,0:T(8,128)S(1)} copy-done((f32[128,128]{1,0:T(8,128)S(1)}, f32[128,128]{1,0:T(8,128)}, u32[]{:S(2)}) %copy-start.4) | copy-done | bytes 65560
  3.4 0.0 copy-start.5
  3.4 0.8 %copy-done.5 = f32[128,128]{1,0:T(8,128)S(1)} copy-done((f32[128,128]{1,0:T(8,128)S(1)}, f32[128,128]{1,0:T(8,128)}, u32[]{:S(2)}) %copy-start.5) | copy-done | bytes 65560
  4.2 0.0 copy-start.7
  4.2 0.7 copy-done.7
  4.9 0.0 copy-start.8
  4.9 0.7 copy-done.8
  5.6 0.0 copy-start.9
  5.6 0.7 copy-done.9
  6.2 52.6 %scan_core.1 = (f32[128,512]{1,0:T(8,128)S(1)}, f32[128,512]{1,0:T(8,128)S(1)}, f32[2,16,128]{2,1,0:T(8,128)S(1)}) custom-call(f32[128,512]{1,0:T(8,128)S(1)} %copy-done, f32[8,128]{1,0:T(8,128)S(1)} %copy-done.7, f32[8]{0:T(128)S(1)} %copy-done.8, f32[128,128]{1,0:T(8,128)S(1)} %copy-done.4, f32[128,128]{1,0:T(8,128)S(1)} %copy-done.5, f32[8]{0:T(128)S(1)} %copy-done.9, ...), custom_call_target="tpu_custom_call" | custom-call | tf_op jit(solution)/shard_map/scan_core/pallas_call | solution.py:294
  58.8 0.0 copy-start.2
  58.8 0.7 copy-done.2
  59.5 0.0 copy-start.3
  59.5 0.7 copy-done.3
  60.2 0.0 copy-start.6
  60.2 0.6 copy-done.6
  60.8 17.5 %hand_over.1 = (f32[128,512]{1,0:T(8,128)}, f32[128,512]{1,0:T(8,128)}, f32[16,128]{1,0:T(8,128)}, f32[16,128]{1,0:T(8,128)}) custom-call(f32[128,512]{1,0:T(8,128)} %copy-done.2, f32[128,512]{1,0:T(8,128)} %copy-done.3, f32[2,16,128]{2,1,0:T(8,128)} %copy-done.6), custom_call_target="tpu_custom_call" | custom-call | tf_op jit(solution)/shard_map/hand_over/pallas_call | solution.py:318
Async XLA Ops:
  0.6 1.0 %copy-start = (f32[128,512]{1,0:T(8,128)S(1)}, f32[128,512]{1,0:T(8,128)}, u32[]{:S(2)}) copy-start(f32[128,512]{1,0:T(8,128)} %v_hbm.1) | copy-start | bytes 786436
  1.6 0.9 %copy-start.1 = (f32[128,512]{1,0:T(8,128)S(1)}, f32[128,512]{1,0:T(8,128)}, u32[]{:S(2)}) copy-start(f32[128,512]{1,0:T(8,128)} %g_hbm.1) | copy-start | bytes 786436
  2.5 0.8 %copy-start.4 = (f32[128,128]{1,0:T(8,128)S(1)}, f32[128,128]{1,0:T(8,128)}, u32[]{:S(2)}) copy-start(f32[128,128]{1,0:T(8,128)} %b_hbm.1) | copy-start | bytes 196612
  3.4 0.8 %copy-start.5 = (f32[128,128]{1,0:T(8,128)S(1)}, f32[128,128]{1,0:T(8,128)}, u32[]{:S(2)}) copy-start(f32[128,128]{1,0:T(8,128)} %c_hbm.1) | copy-start | bytes 196612
  4.2 0.7 copy-start.7
  4.9 0.7 copy-start.8
  5.6 0.7 copy-start.9
  58.8 0.7 copy-start.2
  59.5 0.7 copy-start.3
  60.2 0.6 copy-start.6

commit v2 on v1

--- a/solution.py
+++ b/solution.py
@@ -29,10 +29,10 @@
 
 
 def core_kernel(
-    v_hbm, step_hbm, rate, b_hbm, c_hbm, gain, g_hbm,
-    out_hbm, gv_hbm, maps_out,
-    v, g, step, bmap, cmap,
-    out_acc, gv_acc, from_w, end_w, gf_h, gf_l, xe_h, xe_l, local_maps,
+    v_hbm, step_hbm, rate_hbm, b_hbm, c_hbm, gain_hbm, g_hbm,
+    out_hbm, gv_hbm, maps_hbm,
+    v, g, step, bmap, cmap, rate, gain,
+    out_acc, gv_acc, maps, from_w, end_w, gf_h, gf_l, xe_h, xe_l, local_maps,
     xs_f, xs_b, xr_f, xr_b, zs_f, zs_b, zr_f, zr_b, ys_f, ys_b, enter, leave, ws_f, ws_b, inc, fol, rs_s, rs_r,
     load_sem, x1_s, x1_r, z1_s, z1_r, z2_s, z2_r, x2_s, x2_r, rs_ss, rs_rs, out_sem,
 ):
@@ -56,7 +56,7 @@
     loads = [
         pltpu.make_async_copy(src, dst, load_sem.at[i])
         for i, (src, dst) in enumerate(
-            ((step_hbm, step), (b_hbm, bmap), (c_hbm, cmap), (v_hbm, v), (g_hbm, g))
+            ((step_hbm, step), (rate_hbm, rate), (b_hbm, bmap), (c_hbm, cmap), (v_hbm, v), (g_hbm, g), (gain_hbm, gain))
         )
     ]
     for load in loads:
@@ -69,6 +69,7 @@
     upper = rows <= lanes
 
     loads[0].wait()
+    loads[1].wait()
     steps = step[...]
     head_rows = lax.broadcasted_iota(jnp.int32, (NH, 128), 0)
     rates = jnp.zeros((NH, 128), F32)
@@ -89,13 +90,14 @@
     def pair(kind, q):
         return jnp.where(first, column(kind, 2 * q), column(kind, 2 * q + 1))
 
-    loads[1].wait()
     loads[2].wait()
+    loads[3].wait()
     b_all, c_all = bmap[...], cmap[...]
     b2, c2 = split(b_all), split(c_all)
     bt2, ct2 = split(b_all.T), split(c_all.T)
-    loads[3].wait()
     loads[4].wait()
+    loads[5].wait()
+    loads[6].wait()
 
     scaled = []
     for q in range(NX):
@@ -112,6 +114,54 @@
         xs_f[q, 0:128, :] = dot3(bt2, xe)
         xs_f[q, 128:129, :] = start[127:128, :]
         xs_b[q] = dot3(ct2, gf)
+
+    pl.semaphore_wait(barrier, len(partners))
+
+    def send(src, dst, send_sem, recv_sem, partner):
+        copy = pltpu.make_async_remote_copy(
+            src_ref=src, dst_ref=dst, send_sem=send_sem, recv_sem=recv_sem, device_id=partner, device_id_type=MESH
+        )
+        copy.start()
+        return copy
+
+    sent = []
+
+    x1 = []
+    for i, (source, target) in enumerate(((xs_f, xr_f), (xs_b, xr_b))):
+        x1.append([
+            send(source.at[lax.rem(mx + d, NX)], target.at[mx], x1_s.at[i, d - 1], x1_r.at[i, d - 1], at_x(d))
+            for d in FAR_X
+        ])
+        target[mx] = source[mx]
+    sent += x1[0] + x1[1]
+
+    z1 = []
+    for copy in x1[0]:
+        copy.wait_recv()
+    decays = [xr_f[k, 128:129, :] for k in range(NX)]
+    acc = xr_f[0, 0:128, :]
+    for k in range(1, NX):
+        acc = acc * decays[k] + xr_f[k, 0:128, :]
+    plane = decays[0] * decays[1] * decays[2] * decays[3]
+    for j in range(NZ):
+        zs_f[j, 0:8, :] = acc[8 * j : 8 * j + 8, :]
+        zs_f[j, 8:9, :] = plane
+    z1.append([
+        send(zs_f.at[lax.rem(mz + d, NZ)], zr_f.at[mz], z1_s.at[0, d - 1], z1_r.at[0, d - 1], at_z(d)) for d in FAR_Z
+    ])
+    zr_f[mz] = zs_f[mz]
+    for copy in x1[1]:
+        copy.wait_recv()
+    acc = xr_b[NX - 1]
+    for k in range(NX - 2, -1, -1):
+        acc = acc * decays[k] + xr_b[k]
+    for j in range(NZ):
+        zs_b[j] = acc[8 * j : 8 * j + 8, :]
+    z1.append([
+        send(zs_b.at[lax.rem(mz + d, NZ)], zr_b.at[mz], z1_s.at[1, d - 1], z1_r.at[1, d - 1], at_z(d)) for d in FAR_Z
+    ])
+    zr_b[mz] = zs_b[mz]
+    sent += z1[0] + z1[1]
 
     scores, scores_t = dot3(c2, b2, NT), dot3(b2, c2, NT)
     inner = jnp.zeros((128, 128), F32)
@@ -138,54 +188,6 @@
     local_maps[0] = dot3(split(inner), b2)
     local_maps[1] = dot3(split(inner.T), c2)
 
-    pl.semaphore_wait(barrier, len(partners))
-
-    def send(src, dst, send_sem, recv_sem, partner):
-        copy = pltpu.make_async_remote_copy(
-            src_ref=src, dst_ref=dst, send_sem=send_sem, recv_sem=recv_sem, device_id=partner, device_id_type=MESH
-        )
-        copy.start()
-        return copy
-
-    sent = []
-
-    x1 = []
-    for i, (source, target) in enumerate(((xs_f, xr_f), (xs_b, xr_b))):
-        x1.append([
-            send(source.at[lax.rem(mx + d, NX)], target.at[mx], x1_s.at[i, d - 1], x1_r.at[i, d - 1], at_x(d))
-            for d in FAR_X
-        ])
-        target[mx] = source[mx]
-    sent += x1[0] + x1[1]
-
-    z1 = []
-    for copy in x1[0]:
-        copy.wait_recv()
-    decays = [xr_f[k, 128:129, :] for k in range(NX)]
-    acc = xr_f[0, 0:128, :]
-    for k in range(1, NX):
-        acc = acc * decays[k] + xr_f[k, 0:128, :]
-    plane = decays[0] * decays[1] * decays[2] * decays[3]
-    for j in range(NZ):
-        zs_f[j, 0:8, :] = acc[8 * j : 8 * j + 8, :]
-        zs_f[j, 8:9, :] = plane
-    z1.append([
-        send(zs_f.at[lax.rem(mz + d, NZ)], zr_f.at[mz], z1_s.at[0, d - 1], z1_r.at[0, d - 1], at_z(d)) for d in FAR_Z
-    ])
-    zr_f[mz] = zs_f[mz]
-    for copy in x1[1]:
-        copy.wait_recv()
-    acc = xr_b[NX - 1]
-    for k in range(NX - 2, -1, -1):
-        acc = acc * decays[k] + xr_b[k]
-    for j in range(NZ):
-        zs_b[j] = acc[8 * j : 8 * j + 8, :]
-    z1.append([
-        send(zs_b.at[lax.rem(mz + d, NZ)], zr_b.at[mz], z1_s.at[1, d - 1], z1_r.at[1, d - 1], at_z(d)) for d in FAR_Z
-    ])
-    zr_b[mz] = zs_b[mz]
-    sent += z1[0] + z1[1]
-
     z2 = []
     mine_rows = pl.ds(pl.multiple_of(mz * 8, 8), 8)
     for copy in z1[0]:
@@ -243,16 +245,15 @@
         (fol, b2, xe_h, xe_l, end_w, gv_acc, gv_hbm),
     )
     for i, (carried, map2, w_h, w_l, weight, acc_ref, hbm) in enumerate(plans):
-        for copy in x2[i]:
-            copy.wait_recv()
         grad = local_maps[i]
-        for q in range(NX):
+        states = []
+        for copy, d in zip([None] + x2[i], (0,) + FAR_X):
+            if copy is not None:
+                copy.wait_recv()
+            q = lax.rem(mx + NX - d, NX)
             state2 = split(carried[q])
-            acc_ref[q] = acc_ref[q] + weight[q] * dot3(map2, state2)
+            states.append((q, state2))
             grad = grad + dot3((w_h[q], w_l[q]), state2, NT)
-            store = pltpu.make_async_copy(acc_ref.at[q], hbm.at[:, pl.ds(q * 128, 128)], out_sem.at[i, q])
-            store.start()
-            stores.append(store)
         for k in range(NH):
             rs_s[i, k] = grad[16 * k : 16 * k + 16, :]
         rs.append([
@@ -260,6 +261,12 @@
             for d in FAR_H
         ])
         rs_r[i, head] = rs_s[i, head]
+        for n, (q, state2) in enumerate(states):
+            acc_ref[q] = acc_ref[q] + weight[q] * dot3(map2, state2)
+            cols = pl.ds(pl.multiple_of(q * 128, 128), 128)
+            store = pltpu.make_async_copy(acc_ref.at[q], hbm.at[:, cols], out_sem.at[i, n])
+            store.start()
+            stores.append(store)
     sent += rs[0] + rs[1]
     for i in range(2):
         for copy in rs[i]:
@@ -267,27 +274,33 @@
         whole = rs_r[i, 0]
         for k in range(1, NH):
             whole = whole + rs_r[i, k]
-        maps_out[i] = whole
+        maps[i] = whole
+        store = pltpu.make_async_copy(maps.at[i], maps_hbm.at[i], out_sem.at[i, NX])
+        store.start()
+        stores.append(store)
     for copy in stores:
         copy.wait()
     for copy in sent:
         copy.wait_send()
 
 
-def hand_kernel(out_in, gv_in, maps_in, out, gv, gi, go, sem):
-    copies = [
-        pltpu.make_async_copy(src, dst, sem.at[i])
-        for i, (src, dst) in enumerate(((out_in, out), (gv_in, gv), (maps_in.at[1], gi), (maps_in.at[0], go)))
-    ]
-    for copy in copies:
+def hand_kernel(out_in, gv_in, maps_in, out, gv, gi, go, wide, small, sem):
+    pairs = (
+        (out_in, wide.at[0], out), (gv_in, wide.at[1], gv), (maps_in.at[1], small.at[1], gi), (maps_in.at[0], small.at[0], go)
+    )
+    loads = [pltpu.make_async_copy(src, via, sem.at[0, i]) for i, (src, via, _) in enumerate(pairs)]
+    stores = [pltpu.make_async_copy(via, dst, sem.at[1, i]) for i, (_, via, dst) in enumerate(pairs)]
+    for copy in loads:
         copy.start()
-    for copy in copies:
+    for load, store in zip(loads, stores):
+        load.wait()
+        store.start()
+    for copy in stores:
         copy.wait()
 
 
 def shards(values, step_size, decay_rate, input_map, output_map, skip_gain, grad_output):
-    anywhere = pl.BlockSpec(memory_space=pl.ANY)
-    scalars = pl.BlockSpec(memory_space=pltpu.SMEM)
+    far = pl.BlockSpec(memory_space=pltpu.HBM)
     vmem = lambda *shape, dtype=F32: pltpu.VMEM(shape, dtype)
     dma = lambda *shape: pltpu.SemaphoreType.DMA(shape)
     full = jax.ShapeDtypeStruct(values.shape, F32)
@@ -295,11 +308,12 @@
         core_kernel,
         name="scan_core",
         out_shape=(full, full, jax.ShapeDtypeStruct((2, 16, 128), F32)),
-        in_specs=[anywhere, anywhere, scalars, anywhere, anywhere, scalars, anywhere],
-        out_specs=(anywhere, anywhere, pl.BlockSpec(memory_space=pltpu.VMEM)),
+        in_specs=[far] * 7,
+        out_specs=(far,) * 3,
         scratch_shapes=[
             vmem(128, 512), vmem(128, 512), vmem(8, 128), vmem(128, 128), vmem(128, 128),
-            vmem(4, 128, 128), vmem(4, 128, 128), vmem(4, 128, 128), vmem(4, 128, 128),
+            pltpu.SMEM((8,), F32), pltpu.SMEM((8,), F32),
+            vmem(4, 128, 128), vmem(4, 128, 128), vmem(2, 16, 128), vmem(4, 128, 128), vmem(4, 128, 128),
             vmem(4, 128, 128, dtype=BF16), vmem(4, 128, 128, dtype=BF16),
             vmem(4, 128, 128, dtype=BF16), vmem(4, 128, 128, dtype=BF16), vmem(2, 128, 128),
             vmem(4, 129, 128), vmem(4, 128, 128), vmem(4, 129, 128), vmem(4, 128, 128),
@@ -307,11 +321,11 @@
             vmem(16, 8, 128), vmem(16, 8, 128), vmem(128, 128), vmem(128, 128),
             vmem(4, 128, 128), vmem(4, 128, 128), vmem(4, 128, 128), vmem(4, 128, 128),
             vmem(2, 8, 16, 128), vmem(2, 8, 16, 128),
-            dma(5), dma(2, 3), dma(2, 3), dma(2, 15), dma(2, 15), dma(2, 15), dma(2, 15), dma(2, 3), dma(2, 3),
-            dma(2, 7), dma(2, 7), dma(2, 4),
+            dma(7), dma(2, 3), dma(2, 3), dma(2, 15), dma(2, 15), dma(2, 15), dma(2, 15), dma(2, 3), dma(2, 3),
+            dma(2, 7), dma(2, 7), dma(2, 5),
         ],
         compiler_params=pltpu.CompilerParams(
-            collective_id=0, has_side_effects=True, vmem_limit_bytes=32 * 1024 * 1024
+            collective_id=0, has_side_effects=True, vmem_limit_bytes=60 * 1024 * 1024
         ),
     )(values, step_size, decay_rate, input_map, output_map, skip_gain, grad_output)
     piece = jax.ShapeDtypeStruct((16, 128), F32)
@@ -319,9 +333,9 @@
         hand_kernel,
         name="hand_over",
         out_shape=(full, full, piece, piece),
-        in_specs=[anywhere] * 3,
-        out_specs=(anywhere,) * 4,
-        scratch_shapes=[pltpu.SemaphoreType.DMA((4,))],
+        in_specs=[far] * 3,
+        out_specs=(far,) * 4,
+        scratch_shapes=[vmem(2, 128, 512), vmem(2, 16, 128), dma(2, 4)],
     )(out, gv, maps)
 
 

time: 78.7 us -> 54.5 us (0.69)
  Pallas kernels: 70.1 us -> 53.7 us
  local copies, waits for them, and re-layouts: 7.58 us -> 0 us
    pallas_call x1, Pallas kernels: 17.5 us -> 1.81 us  [shards(): pl.pallas_call(hand_kernel, name='hand_over', out_shape=(full, full, piec...]
    unnamed x20 -> x0, local copies, waits for them, and re-layouts: 7.58 us -> none
where the time goes in v2:
time: 54.5 us; the launch traced here: 54.3 us
  Pallas kernels  53.7 us (99%)
  between operations  0.64 us (1%)
    pallas_call x1, Pallas kernels, shards(): pl.pallas_call(core_kernel, name='scan_core', out_shape=(full, full, jax....  51.9 us
    pallas_call x1, Pallas kernels, shards(): pl.pallas_call(hand_kernel, name='hand_over', out_shape=(full, full, piec...  1.81 us

profile of v2, /device:TPU:1, one launch (start us, length us, event | category | flops | bytes accessed | tf_op | source)
XLA Modules:
  0.0 54.3 jit_solution(9986613823262337504)
XLA Ops:
  0.6 51.9 %scan_core.1 = (f32[128,512]{1,0:T(8,128)}, f32[128,512]{1,0:T(8,128)}, f32[2,16,128]{2,1,0:T(8,128)}) custom-call(f32[128,512]{1,0:T(8,128)} %v_hbm.1, f32[8,128]{1,0:T(8,128)} %step_hbm.1, f32[8]{0:T(128)} %rate_hbm.1, f32[128,128]{1,0:T(8,128)} %b_hbm.1, f32[128,128]{1,0:T(8,128)} %c_hbm.1, f32[8]{0:T(128)} %gain_hbm.1, f32[128,512]{1,0:T(8,128)} %g_hbm.1), custom_call_target="tpu_custom_call" | custom-call | tf_op jit(solution)/shard_map/scan_core/pallas_call | solution.py:307
  52.5 1.8 %hand_over.1 = (f32[128,512]{1,0:T(8,128)}, f32[128,512]{1,0:T(8,128)}, f32[16,128]{1,0:T(8,128)}, f32[16,128]{1,0:T(8,128)}) custom-call(f32[128,512]{1,0:T(8,128)} %get-tuple-element.7.out_in, f32[128,512]{1,0:T(8,128)} %get-tuple-element.8.gv_in, f32[2,16,128]{2,1,0:T(8,128)} %get-tuple-element.9.maps_in), custom_call_target="tpu_custom_call" | custom-call | tf_op jit(solution)/shard_map/hand_over/pallas_call | solution.py:332

commit v3 on v2

--- a/solution.py
+++ b/solution.py
@@ -11,6 +11,7 @@
 F32, BF16 = jnp.float32, jnp.bfloat16
 NX, NZ, NH = 4, 16, 8
 FAR_Z = (8, 7, 9, 6, 10, 5, 11, 4, 12, 3, 13, 2, 14, 1, 15)
+NEAR_Z = (4, 12, 3, 13, 2, 14, 1, 15)
 FAR_X = (2, 1, 3)
 FAR_H = (4, 5, 3, 6, 2, 7, 1)
 NN = (((1,), (0,)), ((), ()))
@@ -34,7 +35,7 @@
     v, g, step, bmap, cmap, rate, gain,
     out_acc, gv_acc, maps, from_w, end_w, gf_h, gf_l, xe_h, xe_l, local_maps,
     xs_f, xs_b, xr_f, xr_b, zs_f, zs_b, zr_f, zr_b, ys_f, ys_b, enter, leave, ws_f, ws_b, inc, fol, rs_s, rs_r,
-    load_sem, x1_s, x1_r, z1_s, z1_r, z2_s, z2_r, x2_s, x2_r, rs_ss, rs_rs, out_sem,
+    reach, load_sem, x1_s, x1_r, z1_s, z1_r, z2_s, z2_r, x2_s, x2_r, rs_ss, rs_rs, out_sem,
 ):
     ctx, head = lax.axis_index("ctx"), lax.axis_index("head")
     mz, mx = ctx // NX, ctx % NX
@@ -49,7 +50,7 @@
         return (ctx, lax.rem(head + d, NH))
 
     barrier = pltpu.get_barrier_semaphore()
-    partners = [at_z(d) for d in FAR_Z] + [at_h(d) for d in FAR_H] + [at_x(d) for d in FAR_X]
+    partners = [at_z(d) for d in NEAR_Z] + [at_h(d) for d in FAR_H] + [at_x(d) for d in FAR_X]
     for partner in partners:
         pl.semaphore_signal(barrier, inc=1, device_id=partner, device_id_type=MESH)
 
@@ -116,6 +117,8 @@
         xs_b[q] = dot3(ct2, gf)
 
     pl.semaphore_wait(barrier, len(partners))
+    for d in (4, 12):
+        pl.semaphore_signal(reach, inc=1, device_id=at_z(d), device_id_type=MESH)
 
     def send(src, dst, send_sem, recv_sem, partner):
         copy = pltpu.make_async_remote_copy(
@@ -146,6 +149,7 @@
     for j in range(NZ):
         zs_f[j, 0:8, :] = acc[8 * j : 8 * j + 8, :]
         zs_f[j, 8:9, :] = plane
+    pl.semaphore_wait(reach, 2)
     z1.append([
         send(zs_f.at[lax.rem(mz + d, NZ)], zr_f.at[mz], z1_s.at[0, d - 1], z1_r.at[0, d - 1], at_z(d)) for d in FAR_Z
     ])
@@ -321,7 +325,7 @@
             vmem(16, 8, 128), vmem(16, 8, 128), vmem(128, 128), vmem(128, 128),
             vmem(4, 128, 128), vmem(4, 128, 128), vmem(4, 128, 128), vmem(4, 128, 128),
             vmem(2, 8, 16, 128), vmem(2, 8, 16, 128),
-            dma(7), dma(2, 3), dma(2, 3), dma(2, 15), dma(2, 15), dma(2, 15), dma(2, 15), dma(2, 3), dma(2, 3),
+            pltpu.SemaphoreType.REGULAR, dma(7), dma(2, 3), dma(2, 3), dma(2, 15), dma(2, 15), dma(2, 15), dma(2, 15), dma(2, 3), dma(2, 3),
             dma(2, 7), dma(2, 7), dma(2, 5),
         ],
         compiler_params=pltpu.CompilerParams(

time: 54.5 us -> 50.8 us (0.932)
  Pallas kernels: 53.7 us -> 50 us
    pallas_call x1, Pallas kernels: 51.9 us -> 48.2 us  [shards(): pl.pallas_call(core_kernel, name='scan_core', out_shape=(full, full, jax....]
where the time goes in v3:
time: 50.8 us; the launch traced here: 50.7 us
  Pallas kernels  50 us (98%)
  between operations  0.64 us (1%)
    pallas_call x1, Pallas kernels, shards(): pl.pallas_call(core_kernel, name='scan_core', out_shape=(full, full, jax....  48.2 us
    pallas_call x1, Pallas kernels, shards(): pl.pallas_call(hand_kernel, name='hand_over', out_shape=(full, full, piec...  1.81 us

profile of v3, /device:TPU:1, one launch (start us, length us, event | category | flops | bytes accessed | tf_op | source)
XLA Modules:
  0.0 50.7 jit_solution(5865204837229544117)
XLA Ops:
  0.6 48.2 %scan_core.1 = (f32[128,512]{1,0:T(8,128)}, f32[128,512]{1,0:T(8,128)}, f32[2,16,128]{2,1,0:T(8,128)}) custom-call(f32[128,512]{1,0:T(8,128)} %v_hbm.1, f32[8,128]{1,0:T(8,128)} %step_hbm.1, f32[8]{0:T(128)} %rate_hbm.1, f32[128,128]{1,0:T(8,128)} %b_hbm.1, f32[128,128]{1,0:T(8,128)} %c_hbm.1, f32[8]{0:T(128)} %gain_hbm.1, f32[128,512]{1,0:T(8,128)} %g_hbm.1), custom_call_target="tpu_custom_call" | custom-call | tf_op jit(solution)/shard_map/scan_core/pallas_call | solution.py:311
  48.9 1.8 %hand_over.1 = (f32[128,512]{1,0:T(8,128)}, f32[128,512]{1,0:T(8,128)}, f32[16,128]{1,0:T(8,128)}, f32[16,128]{1,0:T(8,128)}) custom-call(f32[128,512]{1,0:T(8,128)} %get-tuple-element.7.out_in, f32[128,512]{1,0:T(8,128)} %get-tuple-element.8.gv_in, f32[2,16,128]{2,1,0:T(8,128)} %get-tuple-element.9.maps_in), custom_call_target="tpu_custom_call" | custom-call | tf_op jit(solution)/shard_map/hand_over/pallas_call | solution.py:336

commit v4 on v3

v4 whole, which is shorter than its diff:
```python
import functools

import jax
import jax.numpy as jnp
from jax import lax
from jax.experimental import pallas as pl
from jax.experimental.pallas import tpu as pltpu
from jax.sharding import PartitionSpec as P

MESH = pl.DeviceIdType.MESH
F32, BF16 = jnp.float32, jnp.bfloat16
NX, NZ, NH = 4, 16, 8
EARLY = 4
FAR_Z = (8, 7, 9, 6, 10, 5, 11, 4, 12, 3, 13, 2, 14, 1, 15)
NEAR_Z = (4, 12, 3, 13, 2, 14, 1, 15)
FAR_X = (2, 1, 3)
FAR_H = (4, 5, 3, 6, 2, 7, 1)
NN = (((1,), (0,)), ((), ()))
NT = (((1,), (1,)), ((), ()))


def split(x):
    high = x.astype(BF16)
    return high, (x - high.astype(F32)).astype(BF16)


def dot3(a, b, dims=NN):
    (ah, al), (bh, bl) = a, b
    one = functools.partial(lax.dot_general, dimension_numbers=dims, preferred_element_type=F32)
    return one(ah, bh) + (one(al, bh) + one(ah, bl))


def core_kernel(
    v_hbm, step_hbm, rate_hbm, b_hbm, c_hbm, gain_hbm, g_hbm,
    out_hbm, gv_hbm, maps_hbm,
    v, g, step, bmap, cmap, rate, gain,
    out_acc, gv_acc, maps, from_w, end_w, gf_h, gf_l, xe_h, xe_l, local_maps,
    xs_f, xs_b, xr_f, xr_b, zs_f, zs_b, zr_f, zr_b, ys_f, ys_b, enter, leave, handed, total_f, ws_f, ws_b, inc, fol, rs_s, rs_r,
    reach, hand_s, hand_r, load_sem, x1_s, x1_r, z1_s, z1_r, z2_s, z2_r, x2_s, x2_r, rs_ss, rs_rs, out_sem,
):
    ctx, head = lax.axis_index("ctx"), lax.axis_index("head")
    mz, mx = ctx // NX, ctx % NX

    def at_x(d):
        return (mz * NX + lax.rem(mx + d, NX), head)

    def at_z(d):
        return (lax.rem(mz + d, NZ) * NX + mx, head)

    def at_h(d):
        return (ctx, lax.rem(head + d, NH))

    barrier = pltpu.get_barrier_semaphore()
    partners = [at_z(d) for d in NEAR_Z] + [at_h(d) for d in FAR_H] + [at_x(d) for d in FAR_X]
    for partner in partners:
        pl.semaphore_signal(barrier, inc=1, device_id=partner, device_id_type=MESH)

    loads = [
        pltpu.make_async_copy(src, dst, load_sem.at[i])
        for i, (src, dst) in enumerate(
            ((step_hbm, step), (rate_hbm, rate), (b_hbm, bmap), (c_hbm, cmap), (v_hbm, v), (g_hbm, g), (gain_hbm, gain))
        )
    ]
    for load in loads:
        load.start()

    rows = lax.broadcasted_iota(jnp.int32, (128, 128), 0)
    lanes = lax.broadcasted_iota(jnp.int32, (128, 128), 1)
    first = lanes < 64
    lower = rows >= lanes
    upper = rows <= lanes

    loads[0].wait()
    loads[1].wait()
    steps = step[...]
    head_rows = lax.broadcasted_iota(jnp.int32, (NH, 128), 0)
    rates = jnp.zeros((NH, 128), F32)
    for h in range(NH):
        rates = jnp.where(head_rows == h, rate[h], rates)
    cum = lax.dot_general(
        steps * rates, jnp.where(upper, 1.0, 0.0).astype(F32), NN,
        precision=lax.Precision.HIGHEST, preferred_element_type=F32,
    )
    total = cum[:, 127:128]
    table = jnp.concatenate([steps, jnp.exp(cum), jnp.exp(total - cum), cum] + [jnp.zeros((96, 128), F32)], axis=0)
    table = table.T

    def column(kind, h):
        k = kind * NH + h
        return jnp.broadcast_to(table[:, k : k + 1], (128, 128))

    def pair(kind, q):
        return jnp.where(first, column(kind, 2 * q), column(kind, 2 * q + 1))

    loads[2].wait()
    loads[3].wait()
    b_all, c_all = bmap[...], cmap[...]
    b2, c2 = split(b_all), split(c_all)
    bt2, ct2 = split(b_all.T), split(c_all.T)
    loads[4].wait()
    loads[5].wait()
    loads[6].wait()

    scaled = []
    for q in range(NX):
        cols = slice(q * 128, (q + 1) * 128)
        step_w, start, end = pair(0, q), pair(1, q), pair(2, q)
        vq, gq = v[:, cols], g[:, cols]
        x = vq * step_w
        scaled.append(x)
        xe, gf = split(x * end), split(gq * start)
        xe_h[q], xe_l[q] = xe
        gf_h[q], gf_l[q] = gf
        from_w[q] = start
        end_w[q] = end * step_w
        xs_b[q, 0:128, :] = dot3(ct2, gf)
        xs_b[q, 128:129, :] = start[127:128, :]
        xs_f[q, 0:128, :] = dot3(bt2, xe)
        xs_f[q, 128:129, :] = start[127:128, :]

    pl.semaphore_wait(barrier, len(partners))
    for d in (4, 12):
        pl.semaphore_signal(reach, inc=1, device_id=at_z(d), device_id_type=MESH)

    def remote(src, dst, send_sem, recv_sem, partner):
        return pltpu.make_async_remote_copy(
            src_ref=src, dst_ref=dst, send_sem=send_sem, recv_sem=recv_sem, device_id=partner, device_id_type=MESH
        )

    mine_rows = pl.ds(pl.multiple_of(mz * 8, 8), 8)
    xs, xr, zs, zr, ys, carried_in = (xs_b, xs_f), (xr_b, xr_f), (zs_b, zs_f), (zr_b, zr_f), (ys_b, ys_f), (leave, enter)
    ws, states_in = (ws_b, ws_f), (fol, inc)
    x1 = [[
        remote(xs[i].at[lax.rem(mx + d, NX)], xr[i].at[mx], x1_s.at[i, d - 1], x1_r.at[i, d - 1], at_x(d)) for d in FAR_X
    ] for i in range(2)]
    z1 = [[
        remote(zs[i].at[lax.rem(mz + d, NZ)], zr[i].at[mz], z1_s.at[i, d - 1], z1_r.at[i, d - 1], at_z(d)) for d in FAR_Z
    ] for i in range(2)]
    z2 = [[
        remote(
            ys[i].at[lax.rem(mz + d, NZ)], carried_in[i].at[mine_rows], z2_s.at[i, d - 1], z2_r.at[i, d - 1], at_z(d)
        ) for d in FAR_Z
    ] for i in range(2)]
    x2 = [[
        remote(ws[i].at[lax.rem(mx + d, NX)], states_in[i].at[mx], x2_s.at[i, d - 1], x2_r.at[i, d - 1], at_x(d))
        for d in FAR_X
    ] for i in range(2)]
    rs = [[
        remote(rs_s.at[i, lax.rem(head + d, NH)], rs_r.at[i, head], rs_ss.at[i, d - 1], rs_rs.at[i, d - 1], at_h(d))
        for d in FAR_H
    ] for i in range(2)]

    def x1_send(i):
        for copy in x1[i]:
            copy.start()

    @pl.when(mz == 0)
    def _():
        x1_send(1)
        x1_send(0)

    @pl.when(mz != 0)
    def _():
        x1_send(0)
        x1_send(1)

    for i in range(2):
        xr[i][mx] = xs[i][mx]

    def decay(i, k):
        return xr[i][k, 128:129, :]

    def backward_z1():
        for copy in x1[0]:
            copy.wait_recv()
        acc = xr_b[NX - 1, 0:128, :]
        for k in range(NX - 2, -1, -1):
            acc = acc * decay(0, k) + xr_b[k, 0:128, :]
        plane = decay(0, 0) * decay(0, 1) * decay(0, 2) * decay(0, 3)
        for j in range(NZ):
            zs_b[j, 0:8, :] = acc[8 * j : 8 * j + 8, :]
            zs_b[j, 8:9, :] = plane
        pl.semaphore_wait(reach, 2)
        for copy in z1[0]:
            copy.start()
        zr_b[mz] = zs_b[mz]

    def forward_total():
        for copy in x1[1]:
            copy.wait_recv()
        acc = xr_f[0, 0:128, :]
        for k in range(1, NX):
            acc = acc * decay(1, k) + xr_f[k, 0:128, :]
        total_f[...] = acc
        for j in range(NZ):
            zs_f[j] = acc[8 * j : 8 * j + 8, :]

    def forward_z1():
        for copy in z1[1]:
            pl.when(mz != NZ - 1)(copy.start)
        zr_f[mz] = zs_f[mz]

    early = mz < EARLY
    hand_on = remote(handed, enter, hand_s, hand_r, at_z(1))

    def hand_over_state():
        plane = decay(1, 0) * decay(1, 1) * decay(1, 2) * decay(1, 3)
        handed[...] = enter[...] * plane + total_f[...]
        hand_on.start()

    def forward_x2():
        carry = enter[...]
        for k in range(NX):
            ws_f[k] = carry
            if k < NX - 1:
                carry = carry * decay(1, k) + xr_f[k, 0:128, :]
        for copy in x2[1]:
            copy.start()
        inc[mx] = ws_f[mx]

    def backward_x2(carry):
        for k in range(NX - 1, -1, -1):
            ws_b[k] = carry
            if k > 0:
                carry = carry * decay(0, k) + xr_b[k, 0:128, :]
        for copy in x2[0]:
            copy.start()
        fol[mx] = ws_b[mx]

    def last(i):
        carried, map2, w_h, w_l, weight, acc_ref, hbm = (
            (fol, b2, xe_h, xe_l, end_w, gv_acc, gv_hbm),
            (inc, c2, gf_h, gf_l, from_w, out_acc, out_hbm),
        )[i]
        grad = local_maps[i]
        states = []
        for copy, d in zip([None] + x2[i], (0,) + FAR_X):
            if copy is not None:
                copy.wait_recv()
            q = lax.rem(mx + NX - d, NX)
            state2 = split(carried[q])
            states.append((q, state2))
            grad = grad + dot3((w_h[q], w_l[q]), state2, NT)
        for k in range(NH):
            rs_s[i, k] = grad[16 * k : 16 * k + 16, :]
        for copy in rs[i]:
            copy.start()
        rs_r[i, head] = rs_s[i, head]
        for n, (q, state2) in enumerate(states):
            acc_ref[q] = acc_ref[q] + weight[q] * dot3(map2, state2)
            store(i, n, acc_ref.at[q], hbm, q).start()

    def store(i, n, src, hbm, q):
        return pltpu.make_async_copy(src, hbm.at[:, pl.ds(pl.multiple_of(q * 128, 128), 128)], out_sem.at[i, n])

    @pl.when(mz == 0)
    def _():
        forward_total()
        enter[...] = jnp.zeros((128, 128), F32)
        hand_over_state()
        pl.semaphore_wait(reach, 2)
        forward_z1()
        for copy in x1[0]:
            copy.wait_recv()
        forward_x2()

    @pl.when(mz != 0)
    def _():
        backward_z1()
        forward_total()
        pl.when(mz == 1)(hand_on.wait_recv)
        pl.when(mz == 1)(hand_over_state)
        forward_z1()
        pl.when(mz == 1)(forward_x2)

    scores, scores_t = dot3(c2, b2, NT), dot3(b2, c2, NT)
    inner = jnp.zeros((128, 128), F32)
    for q in range(NX):
        cols = slice(q * 128, (q + 1) * 128)
        x, gq = scaled[q], g[:, cols]
        xv, gv2 = split(x), split(gq)
        outs, grads = [], []
        for k in range(2):
            h = 2 * q + k
            mine = first if k == 0 else jnp.logical_not(first)
            gap = column(3, h) - cum[h : h + 1, :]
            kept = jnp.exp(jnp.where(lower, gap, -gap))
            below = jnp.where(lower, kept, 0.0)
            above = jnp.where(upper, kept, 0.0)
            part = split(jnp.where(mine, gq, 0.0))
            inner = inner + dot3(part, xv, NT) * below
            outs.append(dot3(split(scores * below), xv))
            grads.append(dot3(split(scores_t * above), gv2))
        skip = jnp.where(first[0:1], gain[2 * q], gain[2 * q + 1])
        step_w = pair(0, q)
        out_acc[q] = jnp.where(first, outs[0], outs[1]) + skip * v[:, cols]
        gv_acc[q] = step_w * jnp.where(first, grads[0], grads[1]) + skip * gq
    local_maps[1] = dot3(split(inner), b2)
    local_maps[0] = dot3(split(inner.T), c2)

    for copy, d in zip(z1[0], FAR_Z):
        pl.when(lax.rem(mz + NZ - d, NZ) != 0)(copy.wait_recv)
    carry = jnp.zeros((8, 128), F32)
    for j in range(NZ - 1, -1, -1):
        ys_b[j] = carry
        if j > 0:
            carry = carry * zr_b[j, 8:9, :] + zr_b[j, 0:8, :]
    for copy in z2[0]:
        copy.start()
    leave[mine_rows, :] = ys_b[mz]

    @pl.when(mz == 2)
    def _():
        hand_on.wait_recv()
        if EARLY > 3:
            hand_over_state()
        forward_x2()

    for copy, d in zip(z1[1], FAR_Z):
        pl.when(lax.rem(mz + NZ - d, NZ) != NZ - 1)(copy.wait_recv)
    carry = zr_f[0]
    for j in range(1, NZ):
        ys_f[j] = carry
        if j < NZ - 1:
            carry = carry * zr_b[j, 8:9, :] + zr_f[j]
    for copy, d in zip(z2[1], FAR_Z):
        pl.when(lax.rem(mz + d, NZ) >= EARLY)(copy.start)

    if EARLY > 3:

        @pl.when(mz == 3)
        def _():
            hand_on.wait_recv()
            forward_x2()

    for copy in z2[0]:
        copy.wait_recv()
    backward_x2(leave[...])

    @pl.when(early)
    def _():
        last(1)

    @pl.when(jnp.logical_not(early))
    def _():
        enter[mine_rows, :] = ys_f[mz]
        for copy in z2[1]:
            copy.wait_recv()
        forward_x2()

    last(0)

    @pl.when(jnp.logical_not(early))
    def _():
        last(1)

    ends = []
    for i in (1, 0):
        for copy in rs[i]:
            copy.wait_recv()
        whole = rs_r[i, 0]
        for k in range(1, NH):
            whole = whole + rs_r[i, k]
        maps[i] = whole
        ends.append(pltpu.make_async_copy(maps.at[i], maps_hbm.at[i], out_sem.at[i, NX]))
        ends[-1].start()
    for i, (acc_ref, hbm) in enumerate(((gv_acc, gv_hbm), (out_acc, out_hbm))):
        for n in range(NX):
            store(i, n, acc_ref.at[n], hbm, n).wait()
    for copy in ends:
        copy.wait()
    for copy in z1[0]:
        pl.when(mz != 0)(copy.wait_send)
    for copy in z1[1]:
        pl.when(mz != NZ - 1)(copy.wait_send)
    for copy in x1[0] + x1[1] + z2[0] + x2[0] + x2[1] + rs[0] + rs[1]:
        copy.wait_send()
    for copy, d in zip(z2[1], FAR_Z):
        pl.when(lax.rem(mz + d, NZ) >= EARLY)(copy.wait_send)
    pl.when(mz < EARLY - 1)(hand_on.wait_send)


def hand_kernel(out_in, gv_in, maps_in, out, gv, gi, go, wide, small, sem):
    pairs = (
        (out_in, wide.at[0], out), (gv_in, wide.at[1], gv), (maps_in.at[0], small.at[0], gi), (maps_in.at[1], small.at[1], go)
    )
    loads = [pltpu.make_async_copy(src, via, sem.at[0, i]) for i, (src, via, _) in enumerate(pairs)]
    stores = [pltpu.make_async_copy(via, dst, sem.at[1, i]) for i, (_, via, dst) in enumerate(pairs)]
    for copy in loads:
        copy.start()
    for load, store in zip(loads, stores):
        load.wait()
        store.start()
    for copy in stores:
        copy.wait()


def shards(values, step_size, decay_rate, input_map, output_map, skip_gain, grad_output):
    far = pl.BlockSpec(memory_space=pltpu.HBM)
    vmem = lambda *shape, dtype=F32: pltpu.VMEM(shape, dtype)
    dma = lambda *shape: pltpu.SemaphoreType.DMA(shape)
    full = jax.ShapeDtypeStruct(values.shape, F32)
    out, gv, maps = pl.pallas_call(
        core_kernel,
        name="scan_core",
        out_shape=(full, full, jax.ShapeDtypeStruct((2, 16, 128), F32)),
        in_specs=[far] * 7,
        out_specs=(far,) * 3,
        scratch_shapes=[
            vmem(128, 512), vmem(128, 512), vmem(8, 128), vmem(128, 128), vmem(128, 128),
            pltpu.SMEM((8,), F32), pltpu.SMEM((8,), F32),
            vmem(4, 128, 128), vmem(4, 128, 128), vmem(2, 16, 128), vmem(4, 128, 128), vmem(4, 128, 128),
            vmem(4, 128, 128, dtype=BF16), vmem(4, 128, 128, dtype=BF16),
            vmem(4, 128, 128, dtype=BF16), vmem(4, 128, 128, dtype=BF16), vmem(2, 128, 128),
            vmem(4, 129, 128), vmem(4, 129, 128), vmem(4, 129, 128), vmem(4, 129, 128),
            vmem(16, 8, 128), vmem(16, 9, 128), vmem(16, 8, 128), vmem(16, 9, 128),
            vmem(16, 8, 128), vmem(16, 8, 128), vmem(128, 128), vmem(128, 128), vmem(128, 128), vmem(128, 128),
            vmem(4, 128, 128), vmem(4, 128, 128), vmem(4, 128, 128), vmem(4, 128, 128),
            vmem(2, 8, 16, 128), vmem(2, 8, 16, 128),
            pltpu.SemaphoreType.REGULAR, pltpu.SemaphoreType.DMA, pltpu.SemaphoreType.DMA, dma(7), dma(2, 3), dma(2, 3), dma(2, 15), dma(2, 15), dma(2, 15), dma(2, 15), dma(2, 3), dma(2, 3),
            dma(2, 7), dma(2, 7), dma(2, 5),
        ],
        compiler_params=pltpu.CompilerParams(
            collective_id=0, has_side_effects=True, vmem_limit_bytes=60 * 1024 * 1024
        ),
    )(values, step_size, decay_rate, input_map, output_map, skip_gain, grad_output)
    piece = jax.ShapeDtypeStruct((16, 128), F32)
    return pl.pallas_call(
        hand_kernel,
        name="hand_over",
        out_shape=(full, full, piece, piece),
        in_specs=[far] * 3,
        out_specs=(far,) * 4,
        scratch_shapes=[vmem(2, 128, 512), vmem(2, 16, 128), dma(2, 4)],
    )(out, gv, maps)


def solution(mesh):
    placed = (
        P("ctx", "head"),
        P("head", "ctx"),
        P("head"),
        P("ctx", None),
        P("ctx", None),
        P("head"),
        P("ctx", "head"),
    )
    return jax.shard_map(
        shards,
        mesh=mesh,
        in_specs=placed,
        out_specs=(
            P("ctx", "head"),
            P("ctx", "head"),
            P(("ctx", "head"), None),
            P(("ctx", "head"), None),
        ),
        check_vma=False,
    )
```

time: 50.8 us -> 48.2 us (0.949)
  Pallas kernels: 50 us -> 47.4 us
    pallas_call x1, Pallas kernels: 48.2 us -> 45.6 us  [shards(): pl.pallas_call(core_kernel, name='scan_core', out_shape=(full, full, jax....]
where the time goes in v4:
time: 48.2 us; the launch traced here: 48 us
  Pallas kernels  47.4 us (98%)
  between operations  0.64 us (1%)
    pallas_call x1, Pallas kernels, shards(): pl.pallas_call(core_kernel, name='scan_core', out_shape=(full, full, jax....  45.6 us
    pallas_call x1, Pallas kernels, shards(): pl.pallas_call(hand_kernel, name='hand_over', out_shape=(full, full, piec...  1.81 us

profile of v4, /device:TPU:1, one launch (start us, length us, event | category | flops | bytes accessed | tf_op | source)
XLA Modules:
  0.0 48.0 jit_solution(8378867315594782283)
XLA Ops:
  0.6 45.6 %scan_core.1 = (f32[128,512]{1,0:T(8,128)}, f32[128,512]{1,0:T(8,128)}, f32[2,16,128]{2,1,0:T(8,128)}) custom-call(f32[128,512]{1,0:T(8,128)} %v_hbm.1, f32[8,128]{1,0:T(8,128)} %step_hbm.1, f32[8]{0:T(128)} %rate_hbm.1, f32[128,128]{1,0:T(8,128)} %b_hbm.1, f32[128,128]{1,0:T(8,128)} %c_hbm.1, f32[8]{0:T(128)} %gain_hbm.1, f32[128,512]{1,0:T(8,128)} %g_hbm.1), custom_call_target="tpu_custom_call" | custom-call | tf_op jit(solution)/shard_map/scan_core/pallas_call | solution.py:403
  46.2 1.8 %hand_over.1 = (f32[128,512]{1,0:T(8,128)}, f32[128,512]{1,0:T(8,128)}, f32[16,128]{1,0:T(8,128)}, f32[16,128]{1,0:T(8,128)}) custom-call(f32[128,512]{1,0:T(8,128)} %get-tuple-element.7.out_in, f32[128,512]{1,0:T(8,128)} %get-tuple-element.8.gv_in, f32[2,16,128]{2,1,0:T(8,128)} %get-tuple-element.9.maps_in), custom_call_target="tpu_custom_call" | custom-call | tf_op jit(solution)/shard_map/hand_over/pallas_call | solution.py:428

commit v5 on v4

--- a/solution.py
+++ b/solution.py
@@ -32,10 +32,10 @@
 
 def core_kernel(
     v_hbm, step_hbm, rate_hbm, b_hbm, c_hbm, gain_hbm, g_hbm,
-    out_hbm, gv_hbm, maps_hbm,
+    out_hbm, gv_hbm, rs_r,
     v, g, step, bmap, cmap, rate, gain,
-    out_acc, gv_acc, maps, from_w, end_w, gf_h, gf_l, xe_h, xe_l, local_maps,
-    xs_f, xs_b, xr_f, xr_b, zs_f, zs_b, zr_f, zr_b, ys_f, ys_b, enter, leave, handed, total_f, ws_f, ws_b, inc, fol, rs_s, rs_r,
+    out_acc, gv_acc, from_w, end_w, gf_h, gf_l, xe_h, xe_l, local_maps,
+    xs_f, xs_b, xr_f, xr_b, zs_f, zs_b, zr_f, zr_b, ys_f, ys_b, enter, leave, handed, total_f, ws_f, ws_b, inc, fol, rs_s,
     reach, hand_s, hand_r, load_sem, x1_s, x1_r, z1_s, z1_r, z2_s, z2_r, x2_s, x2_r, rs_ss, rs_rs, out_sem,
 ):
     ctx, head = lax.axis_index("ctx"), lax.axis_index("head")
@@ -245,10 +245,13 @@
             rs_s[i, k] = grad[16 * k : 16 * k + 16, :]
         for copy in rs[i]:
             copy.start()
-        rs_r[i, head] = rs_s[i, head]
+        own_piece(i).start()
         for n, (q, state2) in enumerate(states):
             acc_ref[q] = acc_ref[q] + weight[q] * dot3(map2, state2)
             store(i, n, acc_ref.at[q], hbm, q).start()
+
+    def own_piece(i):
+        return pltpu.make_async_copy(rs_s.at[i, head], rs_r.at[i, head], out_sem.at[i, NX])
 
     def store(i, n, src, hbm, q):
         return pltpu.make_async_copy(src, hbm.at[:, pl.ds(pl.multiple_of(q * 128, 128), 128)], out_sem.at[i, n])
@@ -354,21 +357,12 @@
     def _():
         last(1)
 
-    ends = []
-    for i in (1, 0):
-        for copy in rs[i]:
-            copy.wait_recv()
-        whole = rs_r[i, 0]
-        for k in range(1, NH):
-            whole = whole + rs_r[i, k]
-        maps[i] = whole
-        ends.append(pltpu.make_async_copy(maps.at[i], maps_hbm.at[i], out_sem.at[i, NX]))
-        ends[-1].start()
     for i, (acc_ref, hbm) in enumerate(((gv_acc, gv_hbm), (out_acc, out_hbm))):
         for n in range(NX):
             store(i, n, acc_ref.at[n], hbm, n).wait()
-    for copy in ends:
-        copy.wait()
+        own_piece(i).wait()
+        for copy in rs[i]:
+            copy.wait_recv()
     for copy in z1[0]:
         pl.when(mz != 0)(copy.wait_send)
     for copy in z1[1]:
@@ -380,17 +374,27 @@
     pl.when(mz < EARLY - 1)(hand_on.wait_send)
 
 
-def hand_kernel(out_in, gv_in, maps_in, out, gv, gi, go, wide, small, sem):
-    pairs = (
-        (out_in, wide.at[0], out), (gv_in, wide.at[1], gv), (maps_in.at[0], small.at[0], gi), (maps_in.at[1], small.at[1], go)
-    )
-    loads = [pltpu.make_async_copy(src, via, sem.at[0, i]) for i, (src, via, _) in enumerate(pairs)]
-    stores = [pltpu.make_async_copy(via, dst, sem.at[1, i]) for i, (_, via, dst) in enumerate(pairs)]
+def hand_kernel(out_in, gv_in, pieces_in, out, gv, gi, go, wide, pieces, sums, sem):
+    loads = [
+        pltpu.make_async_copy(src, via, sem.at[0, i])
+        for i, (src, via) in enumerate(((pieces_in, pieces), (out_in, wide.at[0]), (gv_in, wide.at[1])))
+    ]
+    stores = [
+        pltpu.make_async_copy(via, dst, sem.at[1, i])
+        for i, (via, dst) in enumerate(((sums.at[0], gi), (sums.at[1], go), (wide.at[0], out), (wide.at[1], gv)))
+    ]
     for copy in loads:
         copy.start()
-    for load, store in zip(loads, stores):
-        load.wait()
-        store.start()
+    loads[0].wait()
+    for i in range(2):
+        whole = pieces[i, 0]
+        for k in range(1, NH):
+            whole = whole + pieces[i, k]
+        sums[i] = whole
+        stores[i].start()
+    for i in range(2):
+        loads[i + 1].wait()
+        stores[i + 2].start()
     for copy in stores:
         copy.wait()
 
@@ -400,23 +404,23 @@
     vmem = lambda *shape, dtype=F32: pltpu.VMEM(shape, dtype)
     dma = lambda *shape: pltpu.SemaphoreType.DMA(shape)
     full = jax.ShapeDtypeStruct(values.shape, F32)
-    out, gv, maps = pl.pallas_call(
+    out, gv, pieces = pl.pallas_call(
         core_kernel,
         name="scan_core",
-        out_shape=(full, full, jax.ShapeDtypeStruct((2, 16, 128), F32)),
+        out_shape=(full, full, jax.ShapeDtypeStruct((2, NH, 16, 128), F32)),
         in_specs=[far] * 7,
         out_specs=(far,) * 3,
         scratch_shapes=[
             vmem(128, 512), vmem(128, 512), vmem(8, 128), vmem(128, 128), vmem(128, 128),
             pltpu.SMEM((8,), F32), pltpu.SMEM((8,), F32),
-            vmem(4, 128, 128), vmem(4, 128, 128), vmem(2, 16, 128), vmem(4, 128, 128), vmem(4, 128, 128),
+            vmem(4, 128, 128), vmem(4, 128, 128), vmem(4, 128, 128), vmem(4, 128, 128),
             vmem(4, 128, 128, dtype=BF16), vmem(4, 128, 128, dtype=BF16),
             vmem(4, 128, 128, dtype=BF16), vmem(4, 128, 128, dtype=BF16), vmem(2, 128, 128),
             vmem(4, 129, 128), vmem(4, 129, 128), vmem(4, 129, 128), vmem(4, 129, 128),
             vmem(16, 8, 128), vmem(16, 9, 128), vmem(16, 8, 128), vmem(16, 9, 128),
             vmem(16, 8, 128), vmem(16, 8, 128), vmem(128, 128), vmem(128, 128), vmem(128, 128), vmem(128, 128),
             vmem(4, 128, 128), vmem(4, 128, 128), vmem(4, 128, 128), vmem(4, 128, 128),
-            vmem(2, 8, 16, 128), vmem(2, 8, 16, 128),
+            vmem(2, 8, 16, 128),
             pltpu.SemaphoreType.REGULAR, pltpu.SemaphoreType.DMA, pltpu.SemaphoreType.DMA, dma(7), dma(2, 3), dma(2, 3), dma(2, 15), dma(2, 15), dma(2, 15), dma(2, 15), dma(2, 3), dma(2, 3),
             dma(2, 7), dma(2, 7), dma(2, 5),
         ],
@@ -431,8 +435,8 @@
         out_shape=(full, full, piece, piece),
         in_specs=[far] * 3,
         out_specs=(far,) * 4,
-        scratch_shapes=[vmem(2, 128, 512), vmem(2, 16, 128), dma(2, 4)],
-    )(out, gv, maps)
+        scratch_shapes=[vmem(2, 128, 512), vmem(2, 8, 16, 128), vmem(2, 16, 128), dma(2, 4)],
+    )(out, gv, pieces)
 
 
 def solution(mesh):

time: 48.2 us -> 47.8 us (level)
  no operation moved by 1% of the time
where the time goes in v5:
time: 47.8 us; the launch traced here: 47.6 us
  Pallas kernels  47 us (98%)
  between operations  0.64 us (1%)
    pallas_call x1, Pallas kernels, shards(): pl.pallas_call(core_kernel, name='scan_core', out_shape=(full, full, jax....  45.1 us
    pallas_call x1, Pallas kernels, shards(): pl.pallas_call(hand_kernel, name='hand_over', out_shape=(full, full, piec...  1.88 us

profile of v5, /device:TPU:1, one launch (start us, length us, event | category | flops | bytes accessed | tf_op | source)
XLA Modules:
  0.0 47.6 jit_solution(7491368679389750066)
XLA Ops:
  0.6 45.1 %scan_core.1 = (f32[128,512]{1,0:T(8,128)}, f32[128,512]{1,0:T(8,128)}, f32[2,8,16,128]{3,2,1,0:T(8,128)}) custom-call(f32[128,512]{1,0:T(8,128)} %v_hbm.1, f32[8,128]{1,0:T(8,128)} %step_hbm.1, f32[8]{0:T(128)} %rate_hbm.1, f32[128,128]{1,0:T(8,128)} %b_hbm.1, f32[128,128]{1,0:T(8,128)} %c_hbm.1, f32[8]{0:T(128)} %gain_hbm.1, f32[128,512]{1,0:T(8,128)} %g_hbm.1), custom_call_target="tpu_custom_call" | custom-call | tf_op jit(solution)/shard_map/scan_core/pallas_call | solution.py:407
  45.8 1.9 %hand_over.1 = (f32[128,512]{1,0:T(8,128)}, f32[128,512]{1,0:T(8,128)}, f32[16,128]{1,0:T(8,128)}, f32[16,128]{1,0:T(8,128)}) custom-call(f32[128,512]{1,0:T(8,128)} %get-tuple-element.7.out_in, f32[128,512]{1,0:T(8,128)} %get-tuple-element.8.gv_in, f32[2,8,16,128]{3,2,1,0:T(8,128)} %get-tuple-element.9.pieces_in), custom_call_target="tpu_custom_call" | custom-call | tf_op jit(solution)/shard_map/hand_over/pallas_call | solution.py:432

commit v6 on v5

--- a/solution.py
+++ b/solution.py
@@ -113,8 +113,8 @@
         gf_h[q], gf_l[q] = gf
         from_w[q] = start
         end_w[q] = end * step_w
-        xs_b[q, 0:128, :] = dot3(ct2, gf)
-        xs_b[q, 128:129, :] = start[127:128, :]
+        xs_b[q, 8:136, :] = dot3(ct2, gf)
+        xs_b[q, 0:1, :] = start[127:128, :]
         xs_f[q, 0:128, :] = dot3(bt2, xe)
         xs_f[q, 128:129, :] = start[127:128, :]
 
@@ -128,23 +128,60 @@
         )
 
     mine_rows = pl.ds(pl.multiple_of(mz * 8, 8), 8)
-    xs, xr, zs, zr, ys, carried_in = (xs_b, xs_f), (xr_b, xr_f), (zs_b, zs_f), (zr_b, zr_f), (ys_b, ys_f), (leave, enter)
-    ws, states_in = (ws_b, ws_f), (fol, inc)
+    xs, xr = (xs_b, xs_f), (xr_b, xr_f)
     x1 = [[
-        remote(xs[i].at[lax.rem(mx + d, NX)], xr[i].at[mx], x1_s.at[i, d - 1], x1_r.at[i, d - 1], at_x(d)) for d in FAR_X
-    ] for i in range(2)]
-    z1 = [[
-        remote(zs[i].at[lax.rem(mz + d, NZ)], zr[i].at[mz], z1_s.at[i, d - 1], z1_r.at[i, d - 1], at_z(d)) for d in FAR_Z
-    ] for i in range(2)]
-    z2 = [[
         remote(
-            ys[i].at[lax.rem(mz + d, NZ)], carried_in[i].at[mine_rows], z2_s.at[i, d - 1], z2_r.at[i, d - 1], at_z(d)
-        ) for d in FAR_Z
-    ] for i in range(2)]
+            xs_b.at[lax.rem(mx + d, NX), part], xr_b.at[mx, part], x1_s.at[h, d - 1], x1_r.at[h, d - 1], at_x(d)
+        ) for d in FAR_X
+    ] for h, part in enumerate((slice(0, 72), slice(72, 136)))]
+    x1.append([
+        remote(xs_f.at[lax.rem(mx + d, NX)], xr_f.at[mx], x1_s.at[2, d - 1], x1_r.at[2, d - 1], at_x(d)) for d in FAR_X
+    ])
+    back_rows = pl.ds(pl.multiple_of(mz // 2 * 8 + mz % 2 * 64, 8), 8)
+
+    def half_copies(make, parity):
+        copies = []
+        for m in (4, 3, 5, 2, 6, 1, 7, 0):
+            d = 2 * m + parity
+            copies.append((d, make(d, lax.max(d, 1) - 1)))
+        return copies
+
+    z1b = [half_copies(
+        lambda d, n: remote(zs_b.at[lax.rem(mz + d, NZ)], zr_b.at[mz], z1_s.at[0, n], z1_r.at[0, n], at_z(d)), (mz + h) % 2
+    ) for h in range(2)]
+    z1b_in = [half_copies(
+        lambda d, n: remote(zs_b.at[0], zr_b.at[0], z1_s.at[0, n], z1_r.at[0, n], at_z(d)), (mz + h) % 2
+    ) for h in range(2)]
+    z2b = [remote(
+        ys_b.at[lax.rem(mz + d, NZ)], leave.at[back_rows], z2_s.at[0, d - 1], z2_r.at[0, d - 1], at_z(d)
+    ) for d in FAR_Z]
+    z2b_in = [half_copies(
+        lambda d, n: remote(ys_b.at[0], leave.at[back_rows], z2_s.at[0, n], z2_r.at[0, n], at_z(d)), (mz + h) % 2
+    ) for h in range(2)]
+    z1 = [
+        remote(zs_f.at[lax.rem(mz + d, NZ)], zr_f.at[mz], z1_s.at[1, d - 1], z1_r.at[1, d - 1], at_z(d)) for d in FAR_Z
+    ]
+    z2 = [
+        remote(ys_f.at[lax.rem(mz + d, NZ)], enter.at[mine_rows], z2_s.at[1, d - 1], z2_r.at[1, d - 1], at_z(d))
+        for d in FAR_Z
+    ]
     x2 = [[
-        remote(ws[i].at[lax.rem(mx + d, NX)], states_in[i].at[mx], x2_s.at[i, d - 1], x2_r.at[i, d - 1], at_x(d))
+        remote(ws_b.at[lax.rem(mx + d, NX), part], fol.at[mx, part], x2_s.at[h, d - 1], x2_r.at[h, d - 1], at_x(d))
         for d in FAR_X
-    ] for i in range(2)]
+    ] for h, part in enumerate((slice(0, 64), slice(64, 128)))]
+    x2.append([
+        remote(ws_f.at[lax.rem(mx + d, NX)], inc.at[mx], x2_s.at[2, d - 1], x2_r.at[2, d - 1], at_x(d)) for d in FAR_X
+    ])
+    x2_out = []
+    for h, part in enumerate((slice(0, 64), slice(64, 128), slice(0, 128))):
+        src, dst, outs = (ws_b, ws_b, ws_f)[h], (fol, fol, inc)[h], []
+        for t in (0, 1, 3, 2):
+            n = lax.rem(t + NX - 1 - mx + NX, NX)
+            outs.append((t, remote(
+                src.at[t, part], dst.at[mx, part], x2_s.at[h, lax.min(n, 2)], x2_r.at[h, lax.min(n, 2)],
+                (mz * NX + t, head),
+            )))
+        x2_out.append(outs)
     rs = [[
         remote(rs_s.at[i, lax.rem(head + d, NH)], rs_r.at[i, head], rs_ss.at[i, d - 1], rs_rs.at[i, d - 1], at_h(d))
         for d in FAR_H
@@ -156,37 +193,44 @@
 
     @pl.when(mz == 0)
     def _():
-        x1_send(1)
-        x1_send(0)
-
-    @pl.when(mz != 0)
-    def _():
+        x1_send(2)
         x1_send(0)
         x1_send(1)
 
+    @pl.when(mz != 0)
+    def _():
+        x1_send(0)
+        x1_send(1)
+        x1_send(2)
+
     for i in range(2):
         xr[i][mx] = xs[i][mx]
 
     def decay(i, k):
-        return xr[i][k, 128:129, :]
+        return xr_b[k, 0:1, :] if i == 0 else xr_f[k, 128:129, :]
 
     def backward_z1():
-        for copy in x1[0]:
-            copy.wait_recv()
-        acc = xr_b[NX - 1, 0:128, :]
-        for k in range(NX - 2, -1, -1):
-            acc = acc * decay(0, k) + xr_b[k, 0:128, :]
-        plane = decay(0, 0) * decay(0, 1) * decay(0, 2) * decay(0, 3)
-        for j in range(NZ):
-            zs_b[j, 0:8, :] = acc[8 * j : 8 * j + 8, :]
-            zs_b[j, 8:9, :] = plane
-        pl.semaphore_wait(reach, 2)
-        for copy in z1[0]:
-            copy.start()
+        for h in range(2):
+            for copy in x1[h]:
+                copy.wait_recv()
+            rows_in = slice(8 + 64 * h, 72 + 64 * h)
+            acc = xr_b[NX - 1, rows_in, :]
+            for k in range(NX - 2, -1, -1):
+                acc = acc * decay(0, k) + xr_b[k, rows_in, :]
+            plane = decay(0, 0) * decay(0, 1) * decay(0, 2) * decay(0, 3)
+            for j in range(NZ // 2):
+                zs_b[2 * j + h, 0:8, :] = acc[8 * j : 8 * j + 8, :]
+                zs_b[2 * j + h, 8:9, :] = plane
+            if h == 0:
+                pl.semaphore_wait(reach, 2)
+            for d, copy in z1b[h][:-1]:
+                copy.start()
+            d, copy = z1b[h][-1]
+            pl.when(d != 0)(copy.start)
         zr_b[mz] = zs_b[mz]
 
     def forward_total():
-        for copy in x1[1]:
+        for copy in x1[2]:
             copy.wait_recv()
         acc = xr_f[0, 0:128, :]
         for k in range(1, NX):
@@ -196,7 +240,7 @@
             zs_f[j] = acc[8 * j : 8 * j + 8, :]
 
     def forward_z1():
-        for copy in z1[1]:
+        for copy in z1:
             pl.when(mz != NZ - 1)(copy.start)
         zr_f[mz] = zs_f[mz]
 
@@ -214,18 +258,20 @@
             ws_f[k] = carry
             if k < NX - 1:
                 carry = carry * decay(1, k) + xr_f[k, 0:128, :]
-        for copy in x2[1]:
-            copy.start()
+        for t, copy in x2_out[2]:
+            pl.when(mx != t)(copy.start)
         inc[mx] = ws_f[mx]
 
-    def backward_x2(carry):
+    def backward_x2(h):
+        part, rows_in = slice(64 * h, 64 * h + 64), slice(8 + 64 * h, 72 + 64 * h)
+        carry = leave[part, :]
         for k in range(NX - 1, -1, -1):
-            ws_b[k] = carry
+            ws_b[k, part, :] = carry
             if k > 0:
-                carry = carry * decay(0, k) + xr_b[k, 0:128, :]
-        for copy in x2[0]:
-            copy.start()
-        fol[mx] = ws_b[mx]
+                carry = carry * decay(0, k) + xr_b[k, rows_in, :]
+        for t, copy in x2_out[h]:
+            pl.when(mx != t)(copy.start)
+        fol[mx, part, :] = ws_b[mx, part, :]
 
     def last(i):
         carried, map2, w_h, w_l, weight, acc_ref, hbm = (
@@ -234,17 +280,20 @@
         )[i]
         grad = local_maps[i]
         states = []
-        for copy, d in zip([None] + x2[i], (0,) + FAR_X):
-            if copy is not None:
-                copy.wait_recv()
+        for n, d in enumerate((0,) + FAR_X):
+            if d > 0:
+                for copies in (x2[:2], x2[2:])[i]:
+                    copies[n - 1].wait_recv()
             q = lax.rem(mx + NX - d, NX)
             state2 = split(carried[q])
             states.append((q, state2))
             grad = grad + dot3((w_h[q], w_l[q]), state2, NT)
         for k in range(NH):
             rs_s[i, k] = grad[16 * k : 16 * k + 16, :]
-        for copy in rs[i]:
-            copy.start()
+        for t in (1, 0, 3, 2, 5, 7, 4, 6):
+            n = lax.min(lax.rem(t + 2 * NH - 1 - head, NH), NH - 2)
+            copy = remote(rs_s.at[i, t], rs_r.at[i, head], rs_ss.at[i, n], rs_rs.at[i, n], (ctx, t))
+            pl.when(head != t)(copy.start)
         own_piece(i).start()
         for n, (q, state2) in enumerate(states):
             acc_ref[q] = acc_ref[q] + weight[q] * dot3(map2, state2)
@@ -263,7 +312,7 @@
         hand_over_state()
         pl.semaphore_wait(reach, 2)
         forward_z1()
-        for copy in x1[0]:
+        for copy in x1[0] + x1[1]:
             copy.wait_recv()
         forward_x2()
 
@@ -301,16 +350,19 @@
     local_maps[1] = dot3(split(inner), b2)
     local_maps[0] = dot3(split(inner.T), c2)
 
-    for copy, d in zip(z1[0], FAR_Z):
-        pl.when(lax.rem(mz + NZ - d, NZ) != 0)(copy.wait_recv)
+    for h in range(2):
+        for d, copy in z1b_in[h]:
+            pl.when(jnp.logical_and(d != 0, lax.rem(mz + NZ - d, NZ) != 0))(copy.wait_recv)
     carry = jnp.zeros((8, 128), F32)
     for j in range(NZ - 1, -1, -1):
         ys_b[j] = carry
         if j > 0:
             carry = carry * zr_b[j, 8:9, :] + zr_b[j, 0:8, :]
-    for copy in z2[0]:
-        copy.start()
-    leave[mine_rows, :] = ys_b[mz]
+    for t in (0, 1, 2, 3, 4, 5, 6, 7, 15, 14, 13, 12, 8, 11, 10, 9):
+        n = lax.min(lax.rem(t + 2 * NZ - 1 - mz, NZ), NZ - 2)
+        copy = remote(ys_b.at[t], leave.at[back_rows], z2_s.at[0, n], z2_r.at[0, n], (t * NX + mx, head))
+        pl.when(mz != t)(copy.start)
+    leave[back_rows, :] = ys_b[mz]
 
     @pl.when(mz == 2)
     def _():
@@ -319,14 +371,14 @@
             hand_over_state()
         forward_x2()
 
-    for copy, d in zip(z1[1], FAR_Z):
+    for copy, d in zip(z1, FAR_Z):
         pl.when(lax.rem(mz + NZ - d, NZ) != NZ - 1)(copy.wait_recv)
     carry = zr_f[0]
     for j in range(1, NZ):
         ys_f[j] = carry
         if j < NZ - 1:
             carry = carry * zr_b[j, 8:9, :] + zr_f[j]
-    for copy, d in zip(z2[1], FAR_Z):
+    for copy, d in zip(z2, FAR_Z):
         pl.when(lax.rem(mz + d, NZ) >= EARLY)(copy.start)
 
     if EARLY > 3:
@@ -336,9 +388,12 @@
             hand_on.wait_recv()
             forward_x2()
 
-    for copy in z2[0]:
-        copy.wait_recv()
-    backward_x2(leave[...])
+    for h in range(2):
+        for d, copy in z2b_in[h][:-1]:
+            copy.wait_recv()
+        d, copy = z2b_in[h][-1]
+        pl.when(d != 0)(copy.wait_recv)
+        backward_x2(h)
 
     @pl.when(early)
     def _():
@@ -347,7 +402,7 @@
     @pl.when(jnp.logical_not(early))
     def _():
         enter[mine_rows, :] = ys_f[mz]
-        for copy in z2[1]:
+        for copy in z2:
             copy.wait_recv()
         forward_x2()
 
@@ -363,13 +418,14 @@
         own_piece(i).wait()
         for copy in rs[i]:
             copy.wait_recv()
-    for copy in z1[0]:
-        pl.when(mz != 0)(copy.wait_send)
-    for copy in z1[1]:
+    for h in range(2):
+        for d, copy in z1b[h]:
+            pl.when(jnp.logical_and(mz != 0, d != 0))(copy.wait_send)
+    for copy in z1:
         pl.when(mz != NZ - 1)(copy.wait_send)
-    for copy in x1[0] + x1[1] + z2[0] + x2[0] + x2[1] + rs[0] + rs[1]:
+    for copy in sum(x1 + x2 + rs, []) + z2b:
         copy.wait_send()
-    for copy, d in zip(z2[1], FAR_Z):
+    for copy, d in zip(z2, FAR_Z):
         pl.when(lax.rem(mz + d, NZ) >= EARLY)(copy.wait_send)
     pl.when(mz < EARLY - 1)(hand_on.wait_send)
 
@@ -416,12 +472,12 @@
             vmem(4, 128, 128), vmem(4, 128, 128), vmem(4, 128, 128), vmem(4, 128, 128),
             vmem(4, 128, 128, dtype=BF16), vmem(4, 128, 128, dtype=BF16),
             vmem(4, 128, 128, dtype=BF16), vmem(4, 128, 128, dtype=BF16), vmem(2, 128, 128),
-            vmem(4, 129, 128), vmem(4, 129, 128), vmem(4, 129, 128), vmem(4, 129, 128),
+            vmem(4, 129, 128), vmem(4, 136, 128), vmem(4, 129, 128), vmem(4, 136, 128),
             vmem(16, 8, 128), vmem(16, 9, 128), vmem(16, 8, 128), vmem(16, 9, 128),
             vmem(16, 8, 128), vmem(16, 8, 128), vmem(128, 128), vmem(128, 128), vmem(128, 128), vmem(128, 128),
             vmem(4, 128, 128), vmem(4, 128, 128), vmem(4, 128, 128), vmem(4, 128, 128),
             vmem(2, 8, 16, 128),
-            pltpu.SemaphoreType.REGULAR, pltpu.SemaphoreType.DMA, pltpu.SemaphoreType.DMA, dma(7), dma(2, 3), dma(2, 3), dma(2, 15), dma(2, 15), dma(2, 15), dma(2, 15), dma(2, 3), dma(2, 3),
+            pltpu.SemaphoreType.REGULAR, pltpu.SemaphoreType.DMA, pltpu.SemaphoreType.DMA, dma(7), dma(3, 3), dma(3, 3), dma(2, 15), dma(2, 15), dma(2, 15), dma(2, 15), dma(3, 3), dma(3, 3),
             dma(2, 7), dma(2, 7), dma(2, 5),
         ],
         compiler_params=pltpu.CompilerParams(

time: 47.8 us -> 47.1 us (0.985)
  Pallas kernels: 47 us -> 46.3 us
    pallas_call x1, Pallas kernels: 45.1 us -> 44.4 us  [shards(): pl.pallas_call(core_kernel, name='scan_core', out_shape=(full, full, jax....]
where the time goes in v6:
time: 47.1 us; the launch traced here: 46.9 us
  Pallas kernels  46.3 us (98%)
  between operations  0.64 us (1%)
    pallas_call x1, Pallas kernels, shards(): pl.pallas_call(core_kernel, name='scan_core', out_shape=(full, full, jax....  44.4 us
    pallas_call x1, Pallas kernels, shards(): pl.pallas_call(hand_kernel, name='hand_over', out_shape=(full, full, piec...  1.88 us

profile of v6, /device:TPU:1, one launch (start us, length us, event | category | flops | bytes accessed | tf_op | source)
XLA Modules:
  0.0 46.9 jit_solution(4825513603393026598)
XLA Ops:
  0.6 44.4 %scan_core.1 = (f32[128,512]{1,0:T(8,128)}, f32[128,512]{1,0:T(8,128)}, f32[2,8,16,128]{3,2,1,0:T(8,128)}) custom-call(f32[128,512]{1,0:T(8,128)} %v_hbm.1, f32[8,128]{1,0:T(8,128)} %step_hbm.1, f32[8]{0:T(128)} %rate_hbm.1, f32[128,128]{1,0:T(8,128)} %b_hbm.1, f32[128,128]{1,0:T(8,128)} %c_hbm.1, f32[8]{0:T(128)} %gain_hbm.1, f32[128,512]{1,0:T(8,128)} %g_hbm.1), custom_call_target="tpu_custom_call" | custom-call | tf_op jit(solution)/shard_map/scan_core/pallas_call | solution.py:463
  45.0 1.9 %hand_over.1 = (f32[128,512]{1,0:T(8,128)}, f32[128,512]{1,0:T(8,128)}, f32[16,128]{1,0:T(8,128)}, f32[16,128]{1,0:T(8,128)}) custom-call(f32[128,512]{1,0:T(8,128)} %get-tuple-element.7.out_in, f32[128,512]{1,0:T(8,128)} %get-tuple-element.8.gv_in, f32[2,8,16,128]{3,2,1,0:T(8,128)} %get-tuple-element.9.pieces_in), custom_call_target="tpu_custom_call" | custom-call | tf_op jit(solution)/shard_map/hand_over/pallas_call | solution.py:488

commit v7 on v6

--- a/solution.py
+++ b/solution.py
@@ -280,10 +280,10 @@
         )[i]
         grad = local_maps[i]
         states = []
-        for n, d in enumerate((0,) + FAR_X):
+        for d in (0, 1, 3, 2):
             if d > 0:
                 for copies in (x2[:2], x2[2:])[i]:
-                    copies[n - 1].wait_recv()
+                    copies[FAR_X.index(d)].wait_recv()
             q = lax.rem(mx + NX - d, NX)
             state2 = split(carried[q])
             states.append((q, state2))
@@ -412,22 +412,26 @@
     def _():
         last(1)
 
-    for i, (acc_ref, hbm) in enumerate(((gv_acc, gv_hbm), (out_acc, out_hbm))):
-        for n in range(NX):
-            store(i, n, acc_ref.at[n], hbm, n).wait()
-        own_piece(i).wait()
-        for copy in rs[i]:
-            copy.wait_recv()
     for h in range(2):
         for d, copy in z1b[h]:
             pl.when(jnp.logical_and(mz != 0, d != 0))(copy.wait_send)
     for copy in z1:
         pl.when(mz != NZ - 1)(copy.wait_send)
-    for copy in sum(x1 + x2 + rs, []) + z2b:
+    for copy in sum(x1 + x2, []) + z2b:
         copy.wait_send()
     for copy, d in zip(z2, FAR_Z):
         pl.when(lax.rem(mz + d, NZ) >= EARLY)(copy.wait_send)
     pl.when(mz < EARLY - 1)(hand_on.wait_send)
+    for i, (acc_ref, hbm) in enumerate(((gv_acc, gv_hbm), (out_acc, out_hbm))):
+        for n in range(NX):
+            store(i, n, acc_ref.at[n], hbm, n).wait()
+        own_piece(i).wait()
+    for i in (1, 0):
+        for copy in rs[i]:
+            copy.wait_send()
+    for i in (1, 0):
+        for copy in rs[i]:
+            copy.wait_recv()
 
 
 def hand_kernel(out_in, gv_in, pieces_in, out, gv, gi, go, wide, pieces, sums, sem):

time: 47.1 us -> 46.6 us (0.989)
  Pallas kernels: 46.3 us -> 45.8 us
    pallas_call x1, Pallas kernels: 44.4 us -> 43.9 us  [shards(): pl.pallas_call(core_kernel, name='scan_core', out_shape=(full, full, jax....]
where the time goes in v7:
time: 46.6 us; the launch traced here: 46.4 us
  Pallas kernels  45.8 us (98%)
  between operations  0.64 us (1%)
    pallas_call x1, Pallas kernels, shards(): pl.pallas_call(core_kernel, name='scan_core', out_shape=(full, full, jax....  43.9 us
    pallas_call x1, Pallas kernels, shards(): pl.pallas_call(hand_kernel, name='hand_over', out_shape=(full, full, piec...  1.88 us

profile of v7, /device:TPU:1, one launch (start us, length us, event | category | flops | bytes accessed | tf_op | source)
XLA Modules:
  0.0 46.4 jit_solution(5753962750260841779)
XLA Ops:
  0.6 43.9 %scan_core.1 = (f32[128,512]{1,0:T(8,128)}, f32[128,512]{1,0:T(8,128)}, f32[2,8,16,128]{3,2,1,0:T(8,128)}) custom-call(f32[128,512]{1,0:T(8,128)} %v_hbm.1, f32[8,128]{1,0:T(8,128)} %step_hbm.1, f32[8]{0:T(128)} %rate_hbm.1, f32[128,128]{1,0:T(8,128)} %b_hbm.1, f32[128,128]{1,0:T(8,128)} %c_hbm.1, f32[8]{0:T(128)} %gain_hbm.1, f32[128,512]{1,0:T(8,128)} %g_hbm.1), custom_call_target="tpu_custom_call" | custom-call | tf_op jit(solution)/shard_map/scan_core/pallas_call | solution.py:467
  44.5 1.9 %hand_over.1 = (f32[128,512]{1,0:T(8,128)}, f32[128,512]{1,0:T(8,128)}, f32[16,128]{1,0:T(8,128)}, f32[16,128]{1,0:T(8,128)}) custom-call(f32[128,512]{1,0:T(8,128)} %get-tuple-element.7.out_in, f32[128,512]{1,0:T(8,128)} %get-tuple-element.8.gv_in, f32[2,8,16,128]{3,2,1,0:T(8,128)} %get-tuple-element.9.pieces_in), custom_call_target="tpu_custom_call" | custom-call | tf_op jit(solution)/shard_map/hand_over/pallas_call | solution.py:492

commit v8 on v7

--- a/solution.py
+++ b/solution.py
@@ -201,7 +201,6 @@
     def _():
         x1_send(0)
         x1_send(1)
-        x1_send(2)
 
     for i in range(2):
         xr[i][mx] = xs[i][mx]
@@ -213,6 +212,8 @@
         for h in range(2):
             for copy in x1[h]:
                 copy.wait_recv()
+            if h == 0:
+                x1_send(2)
             rows_in = slice(8 + 64 * h, 72 + 64 * h)
             acc = xr_b[NX - 1, rows_in, :]
             for k in range(NX - 2, -1, -1):

time: 46.6 us -> 46.3 us (level)
  Pallas kernels: 45.8 us -> 45.1 us
    pallas_call x1, Pallas kernels: 43.9 us -> 43.2 us  [shards(): pl.pallas_call(core_kernel, name='scan_core', out_shape=(full, full, jax....]
where the time goes in v8:
time: 46.3 us; the launch traced here: 45.7 us
  Pallas kernels  45.1 us (97%)
  between operations  0.64 us (1%)
    pallas_call x1, Pallas kernels, shards(): pl.pallas_call(core_kernel, name='scan_core', out_shape=(full, full, jax....  43.2 us
    pallas_call x1, Pallas kernels, shards(): pl.pallas_call(hand_kernel, name='hand_over', out_shape=(full, full, piec...  1.88 us

profile of v8, /device:TPU:1, one launch (start us, length us, event | category | flops | bytes accessed | tf_op | source)
XLA Modules:
  0.0 45.7 jit_solution(9140885483783283394)
XLA Ops:
  0.6 43.2 %scan_core.1 = (f32[128,512]{1,0:T(8,128)}, f32[128,512]{1,0:T(8,128)}, f32[2,8,16,128]{3,2,1,0:T(8,128)}) custom-call(f32[128,512]{1,0:T(8,128)} %v_hbm.1, f32[8,128]{1,0:T(8,128)} %step_hbm.1, f32[8]{0:T(128)} %rate_hbm.1, f32[128,128]{1,0:T(8,128)} %b_hbm.1, f32[128,128]{1,0:T(8,128)} %c_hbm.1, f32[8]{0:T(128)} %gain_hbm.1, f32[128,512]{1,0:T(8,128)} %g_hbm.1), custom_call_target="tpu_custom_call" | custom-call | tf_op jit(solution)/shard_map/scan_core/pallas_call | solution.py:468
  43.9 1.9 %hand_over.1 = (f32[128,512]{1,0:T(8,128)}, f32[128,512]{1,0:T(8,128)}, f32[16,128]{1,0:T(8,128)}, f32[16,128]{1,0:T(8,128)}) custom-call(f32[128,512]{1,0:T(8,128)} %get-tuple-element.7.out_in, f32[128,512]{1,0:T(8,128)} %get-tuple-element.8.gv_in, f32[2,8,16,128]{3,2,1,0:T(8,128)} %get-tuple-element.9.pieces_in), custom_call_target="tpu_custom_call" | custom-call | tf_op jit(solution)/shard_map/hand_over/pallas_call | solution.py:493
